TPU v7x, 128 devices: a whole 4x4x4 slice. The times are simulated.
128 devices in a mesh: sta: 16 (over x, z), tpl: 8 (over y, core).
Axes of the slice: x: 4, y: 4, z: 4, core: 2. Of those that a mesh axis runs over, the one named last changes fastest.
Arguments:
- records: bfloat16 [1024, 3, 4480], P(('sta', 'tpl')), may hold values from -6 to 6
- templates: bfloat16 [3072, 10, 3, 200], P(('sta', 'tpl')), may hold values from -6 to 6
- pick_owner: int32 [3072, 10], P(('sta', 'tpl')), may hold values from 0 to 127, all different within a row; in each aligned block of 24 rows (0 to 23, 24 to 47, ...) at most 3 rows name the same one
- pick_local: int32 [3072, 10], P(('sta', 'tpl')), may hold values from 0 to 7
- moveout: int32 [3072, 10], P(('sta', 'tpl')), may hold values from 0 to 127
- channel_mask: int32 [3072, 10, 3], P(('sta', 'tpl')), may hold values 0 or 1
Outputs:
- detection: float32 [3072, 4096], P(('sta', 'tpl'))
Inputs may be any that keep to these rules, and one draw needn't show every extreme that they name: `pick_owner`: each template names 10 different devices; among the templates of one device no device is named more than 3 times, and some device is named exactly 3 times.
All inputs are finite; a program needn't handle non-finite values. No bound on the sum of `channel_mask` on one device may be relied on, other than what follows from the above.
Results may differ from a plain program's by a relative error of at most 0.0029.
Values may be sent and summed in bfloat16 or wider, within the bound.
No kernel may reach another device: no remote copies, remote signals or barrier semaphores. Data moves between devices by JAX's collectives and lax.ppermute only.
A program may use at most 128 MiB of HBM per device.

v0:
```python
import jax
import jax.numpy as jnp
from jax import lax
from jax.sharding import PartitionSpec as P

EPS = 1e-06


def toeplitz_rows(blocks, frame_len):
    group_size, channels, shape_len = blocks.shape
    padded = jnp.concatenate(
        [blocks, jnp.zeros((group_size, channels, frame_len + 1 - shape_len), blocks.dtype)], axis=2
    )
    repeated = jnp.broadcast_to(
        padded[:, :, None, :], (group_size, channels, 128, frame_len + 1)
    ).reshape(group_size, channels, 128 * (frame_len + 1))
    return repeated[:, :, : 128 * frame_len].reshape(group_size, channels, 128, frame_len)


def framed(records, frame_len):
    station_count, channels, record_len = records.shape
    pieces = records.reshape(station_count, channels, record_len // 128, 128)
    spread = frame_len // 128
    block_count = record_len // 128 - spread + 1
    return jnp.concatenate(
        [pieces[:, :, offset : offset + block_count, :] for offset in range(spread)], axis=3
    )


def on_device(records, templates, pick_owner, pick_local, moveout, channel_mask):
    devices = lax.axis_size(("sta", "tpl"))
    own_templates, pick_count, channels, shape_len = templates.shape
    frame_len = 128 + 128 * ((shape_len + 127) // 128)
    lag_count = records.shape[2] - frame_len
    lag_blocks = lag_count // 128
    capacity = max(2, (3 * own_templates * pick_count + 2 * devices - 1) // (2 * devices))
    pick_rows = own_templates * pick_count
    owners = pick_owner.reshape(pick_rows)
    onehot = (owners[:, None] == jnp.arange(devices, dtype=jnp.int32)[None, :]).astype(jnp.int32)
    before = jnp.cumsum(onehot, axis=0) - onehot
    position = owners * capacity + jnp.sum(before * onehot, axis=1)
    outbox = (
        jnp.zeros((devices * capacity, channels * shape_len), templates.dtype)
        .at[position]
        .set(templates.reshape(pick_rows, channels * shape_len))
    )
    details = jnp.concatenate(
        [
            pick_local.reshape(pick_rows, 1),
            channel_mask.reshape(pick_rows, channels),
            moveout.reshape(pick_rows, 1),
        ],
        axis=1,
    )
    labels = jnp.zeros((devices * capacity, channels + 2), jnp.int32).at[position].set(details)
    arrived, arrived_marks = (
        lax.all_to_all(
            outbox.reshape(devices, capacity, channels * shape_len),
            ("sta", "tpl"),
            split_axis=0,
            concat_axis=0,
            tiled=True,
        ),
        lax.all_to_all(
            labels.reshape(devices, capacity, channels + 2),
            ("sta", "tpl"),
            split_axis=0,
            concat_axis=0,
            tiled=True,
        ),
    )
    slot_count = devices * capacity
    frames = framed(records, frame_len)
    squares = jnp.square(frames.astype(jnp.float32))
    offsets = (
        jnp.arange(frame_len, dtype=jnp.int32)[:, None] - jnp.arange(128, dtype=jnp.int32)[None, :]
    )
    band = ((offsets >= 0) & (offsets < shape_len)).astype(jnp.float32)
    energy = jnp.einsum("scbm,mj->scbj", squares, band, precision=lax.Precision.HIGHEST)
    group_size = 64
    source_index = jnp.arange(256, dtype=jnp.int32)[:, None]
    target_index = jnp.arange(128, dtype=jnp.int32)[None, :]

    def correlate(pieces):
        shapes, slot_marks = pieces
        stations = slot_marks[:, 0]
        toeplitz = toeplitz_rows(shapes, frame_len)
        windows = frames[stations]
        numerator = jnp.einsum(
            "gcbm,gcjm->gcbj", windows, toeplitz, preferred_element_type=jnp.float32
        )
        template_power = jnp.sum(jnp.square(shapes.astype(jnp.float32)), axis=2)
        scaled = numerator * lax.rsqrt(template_power[:, :, None, None] * energy[stations] + EPS)
        weights = slot_marks[:, 1 : 1 + channels].astype(jnp.float32)
        traces = jnp.sum(weights[:, :, None, None] * scaled, axis=1).astype(jnp.bfloat16)
        paired = jnp.concatenate(
            [traces[:, :lag_blocks, :], traces[:, 1 : lag_blocks + 1, :]], axis=2
        )
        shifts = slot_marks[:, channels + 1]
        selector = (
            source_index[None, :, :] == target_index[None, :, :] + shifts[:, None, None]
        ).astype(jnp.bfloat16)
        aligned = jnp.einsum("gbi,gij->gbj", paired, selector, preferred_element_type=jnp.float32)
        return aligned.astype(jnp.bfloat16).reshape(group_size, lag_count)

    outgoing = lax.map(
        correlate,
        (
            arrived.reshape(slot_count // group_size, group_size, channels, shape_len),
            arrived_marks.reshape(slot_count // group_size, group_size, channels + 2),
        ),
    )
    returned = lax.all_to_all(
        outgoing.reshape(devices, capacity, lag_count),
        ("sta", "tpl"),
        split_axis=0,
        concat_axis=0,
        tiled=True,
    )
    picked = returned.reshape(slot_count, lag_count)[position].astype(jnp.float32)
    stacked = jnp.sum(picked.reshape(own_templates, pick_count, lag_count), axis=1)
    levels = jnp.sqrt(jnp.mean(stacked * stacked, axis=1, keepdims=True) + EPS)
    return stacked / levels


def solution(mesh):
    return jax.shard_map(
        on_device,
        mesh=mesh,
        in_specs=(
            P(("sta", "tpl"), None, None),
            P(("sta", "tpl"), None, None, None),
            P(("sta", "tpl"), None),
            P(("sta", "tpl"), None),
            P(("sta", "tpl"), None),
            P(("sta", "tpl"), None, None),
        ),
        out_specs=P(("sta", "tpl"), None),
        check_vma=False,
    )
```

profile of v0, /device:TPU:1, one launch (start us, length us, event | category | flops | bytes accessed | tf_op | source)
XLA Modules:
  0.0 626.1 jit_solution(10447739974207164868)
XLA Ops:
  5.2 1.2 scatter_custom_fusion
  7.1 11.5 %all-to-all-start = ((s32[128,3,5]{2,1,0:T(4,128)}), s32[128,3,5]{2,1,0:T(4,128)S(1)}, u32[]{:S(2)}, u32[]{:S(2)}) async-start(s32[128,3,5]{2,1,0:T(4,128)} %reshape.191), calls=%async_computation | async-start | bytes 524288 | tf_op jit(solution)/shard_map/all_to_all | solution.py:64
  18.7 1.2 copy.75
  20.1 1.7 scatter_custom_fusion.1
  21.8 1.1 reshape.137
  22.9 6.5 %all-to-all-done = s32[128,3,5]{2,1,0:T(4,128)S(1)} async-done(((s32[128,3,5]{2,1,0:T(4,128)}), s32[128,3,5]{2,1,0:T(4,128)S(1)}, u32[]{:S(2)}, u32[]{:S(2)}) %all-to-all-start) | async-done | bytes 7712 | tf_op jit(solution)/shard_map/all_to_all | solution.py:64
  29.4 4.8 all-to-all-start.1
  35.7 13.4 %all-to-all-done.1 = bf16[128,3,600]{2,1,0:T(4,128)(2,1)S(1)} async-done(((bf16[128,3,600]{2,1,0:T(4,128)(2,1)}), bf16[128,3,600]{2,1,0:T(4,128)(2,1)S(1)}, u32[]{:S(2)}, u32[]{:S(2)}) %all-to-all-start.1) | async-done | bytes 460832 | tf_op jit(solution)/shard_map/all_to_all | solution.py:57
  49.9 492.2 %while.11 = (s32[]{:T(128)}, bf16[6,64,4096]{2,1,0:T(8,128)(2,1)}, s32[6,64,5]{1,2,0:T(8,128)S(1)}, bf16[8,3,33,384]{3,2,1,0:T(8,128)(2,1)S(1)}, bf16[6,64,3,200...) while((s32[]{:T(128)}, bf16[6,64,4096]{2,1,0:T(8,128)(2,1)}, ...), condition=%wide.region_8.9_spmd.clone, body=%wide.region_5.8_spmd.clone.sunk | while | flops 765437632 | bytes 201262720 | solution.py:106
  49.9 3.9 gather_fusion.1
  53.9 2.7 gather_fusion
  56.7 8.4 %broadcast_in_dim.41 = bf16[64,3,128,385]{3,2,0,1:T(8,128)(2,1)} broadcast(bf16[64,3,385]{2,0,1:T(8,128)(2,1)S(1)} %concatenate.17), dimensions={0,1,3} | broadcast | bytes 19071360 | tf_op jit(solution)/shard_map/while/body/eval_jaxpr/broadcast_in_dim | solution.py:14
  65.1 35.9 %reshape.206 = bf16[64,3,49280]{2,0,1:T(8,128)(2,1)} reshape(bf16[64,3,128,385]{3,2,0,1:T(8,128)(2,1)} %broadcast_in_dim.41) | data formatting | bytes 37847040 | tf_op jit(solution)/shard_map/while/body/eval_jaxpr/reshape | solution.py:16
  101.0 6.4 %slice-done = bf16[64,3,49152]{2,0,1:T(8,128)(2,1)S(1)} async-done(((bf16[64,3,49280]{2,0,1:T(8,128)(2,1)}), bf16[64,3,49152]{2,0,1:T(8,128)(2,1)S(1)}, s32[]{:S(2)}) %slice-start) | async-done | bytes 18874392 | tf_op jit(solution)/shard_map/while/body/eval_jaxpr/slice | solution.py:17
  107.4 7.0 %copy.100 = bf16[24,8,128,384]{3,2,1,0:T(8,128)(2,1)} copy(bf16[24,8,128,384]{3,1,2,0:T(8,128)(2,1)S(1)} %bitcast.51) | data formatting | bytes 37748736 | tf_op jit(solution)/shard_map/while
  114.7 14.0 %multiply_reduce_fusion.6 = bf16[64,33,128]{2,1,0:T(8,128)(2,1)S(1)} fusion(f32[64,3,33,128]{3,2,1,0:T(8,128)} %gather_fusion, f32[64,3]{1,0:T(8,128)S(1)} %copy.98, f32[64,3]{1,0:T(8,128)S(1)} %copy.99, bf16[64,3,33,384]{3,2,1,0:T(8,128)(2,1)} %gather_fusion.1, bf16[64,3,128,384]{3,2,0,1:T(8,128)(2,1)} %bitcast.52), kind=kOutput, calls=%fused_computation.12.clone.1 | convolution fusion | flops 626638848 | bytes 27526656 | tf_op jit(solution)/shard_map/while/body/eval_jaxpr/gcbm,gcjm->gcbj/dot_general | solution.py:89
  129.0 1.9 fusion.51
  132.0 3.9 gather_fusion.1
  135.9 2.7 gather_fusion
  138.7 8.4 %broadcast_in_dim.41 = bf16[64,3,128,385]{3,2,0,1:T(8,128)(2,1)} broadcast(bf16[64,3,385]{2,0,1:T(8,128)(2,1)S(1)} %concatenate.17), dimensions={0,1,3} | broadcast | bytes 19071360 | tf_op jit(solution)/shard_map/while/body/eval_jaxpr/broadcast_in_dim | solution.py:14
  147.2 35.9 %reshape.206 = bf16[64,3,49280]{2,0,1:T(8,128)(2,1)} reshape(bf16[64,3,128,385]{3,2,0,1:T(8,128)(2,1)} %broadcast_in_dim.41) | data formatting | bytes 37847040 | tf_op jit(solution)/shard_map/while/body/eval_jaxpr/reshape | solution.py:16
  183.1 6.4 %slice-done = bf16[64,3,49152]{2,0,1:T(8,128)(2,1)S(1)} async-done(((bf16[64,3,49280]{2,0,1:T(8,128)(2,1)}), bf16[64,3,49152]{2,0,1:T(8,128)(2,1)S(1)}, s32[]{:S(2)}) %slice-start) | async-done | bytes 18874392 | tf_op jit(solution)/shard_map/while/body/eval_jaxpr/slice | solution.py:17
  189.5 7.0 %copy.100 = bf16[24,8,128,384]{3,2,1,0:T(8,128)(2,1)} copy(bf16[24,8,128,384]{3,1,2,0:T(8,128)(2,1)S(1)} %bitcast.51) | data formatting | bytes 37748736 | tf_op jit(solution)/shard_map/while
  196.7 14.0 %multiply_reduce_fusion.6 = bf16[64,33,128]{2,1,0:T(8,128)(2,1)S(1)} fusion(f32[64,3,33,128]{3,2,1,0:T(8,128)} %gather_fusion, f32[64,3]{1,0:T(8,128)S(1)} %copy.98, f32[64,3]{1,0:T(8,128)S(1)} %copy.99, bf16[64,3,33,384]{3,2,1,0:T(8,128)(2,1)} %gather_fusion.1, bf16[64,3,128,384]{3,2,0,1:T(8,128)(2,1)} %bitcast.52), kind=kOutput, calls=%fused_computation.12.clone.1 | convolution fusion | flops 626638848 | bytes 27526656 | tf_op jit(solution)/shard_map/while/body/eval_jaxpr/gcbm,gcjm->gcbj/dot_general | solution.py:89
  211.1 1.9 fusion.51
  214.0 3.9 gather_fusion.1
  218.0 2.7 gather_fusion
  220.8 8.4 %broadcast_in_dim.41 = bf16[64,3,128,385]{3,2,0,1:T(8,128)(2,1)} broadcast(bf16[64,3,385]{2,0,1:T(8,128)(2,1)S(1)} %concatenate.17), dimensions={0,1,3} | broadcast | bytes 19071360 | tf_op jit(solution)/shard_map/while/body/eval_jaxpr/broadcast_in_dim | solution.py:14
  229.2 35.9 %reshape.206 = bf16[64,3,49280]{2,0,1:T(8,128)(2,1)} reshape(bf16[64,3,128,385]{3,2,0,1:T(8,128)(2,1)} %broadcast_in_dim.41) | data formatting | bytes 37847040 | tf_op jit(solution)/shard_map/while/body/eval_jaxpr/reshape | solution.py:16
  265.1 6.4 %slice-done = bf16[64,3,49152]{2,0,1:T(8,128)(2,1)S(1)} async-done(((bf16[64,3,49280]{2,0,1:T(8,128)(2,1)}), bf16[64,3,49152]{2,0,1:T(8,128)(2,1)S(1)}, s32[]{:S(2)}) %slice-start) | async-done | bytes 18874392 | tf_op jit(solution)/shard_map/while/body/eval_jaxpr/slice | solution.py:17
  271.5 7.0 %copy.100 = bf16[24,8,128,384]{3,2,1,0:T(8,128)(2,1)} copy(bf16[24,8,128,384]{3,1,2,0:T(8,128)(2,1)S(1)} %bitcast.51) | data formatting | bytes 37748736 | tf_op jit(solution)/shard_map/while
  278.8 14.0 %multiply_reduce_fusion.6 = bf16[64,33,128]{2,1,0:T(8,128)(2,1)S(1)} fusion(f32[64,3,33,128]{3,2,1,0:T(8,128)} %gather_fusion, f32[64,3]{1,0:T(8,128)S(1)} %copy.98, f32[64,3]{1,0:T(8,128)S(1)} %copy.99, bf16[64,3,33,384]{3,2,1,0:T(8,128)(2,1)} %gather_fusion.1, bf16[64,3,128,384]{3,2,0,1:T(8,128)(2,1)} %bitcast.52), kind=kOutput, calls=%fused_computation.12.clone.1 | convolution fusion | flops 626638848 | bytes 27526656 | tf_op jit(solution)/shard_map/while/body/eval_jaxpr/gcbm,gcjm->gcbj/dot_general | solution.py:89
  293.1 1.9 fusion.51
  296.1 3.9 gather_fusion.1
  300.0 2.7 gather_fusion
  302.8 8.4 %broadcast_in_dim.41 = bf16[64,3,128,385]{3,2,0,1:T(8,128)(2,1)} broadcast(bf16[64,3,385]{2,0,1:T(8,128)(2,1)S(1)} %concatenate.17), dimensions={0,1,3} | broadcast | bytes 19071360 | tf_op jit(solution)/shard_map/while/body/eval_jaxpr/broadcast_in_dim | solution.py:14
  311.2 35.9 %reshape.206 = bf16[64,3,49280]{2,0,1:T(8,128)(2,1)} reshape(bf16[64,3,128,385]{3,2,0,1:T(8,128)(2,1)} %broadcast_in_dim.41) | data formatting | bytes 37847040 | tf_op jit(solution)/shard_map/while/body/eval_jaxpr/reshape | solution.py:16
  347.2 6.4 %slice-done = bf16[64,3,49152]{2,0,1:T(8,128)(2,1)S(1)} async-done(((bf16[64,3,49280]{2,0,1:T(8,128)(2,1)}), bf16[64,3,49152]{2,0,1:T(8,128)(2,1)S(1)}, s32[]{:S(2)}) %slice-start) | async-done | bytes 18874392 | tf_op jit(solution)/shard_map/while/body/eval_jaxpr/slice | solution.py:17
  353.5 7.0 %copy.100 = bf16[24,8,128,384]{3,2,1,0:T(8,128)(2,1)} copy(bf16[24,8,128,384]{3,1,2,0:T(8,128)(2,1)S(1)} %bitcast.51) | data formatting | bytes 37748736 | tf_op jit(solution)/shard_map/while
  360.8 14.0 %multiply_reduce_fusion.6 = bf16[64,33,128]{2,1,0:T(8,128)(2,1)S(1)} fusion(f32[64,3,33,128]{3,2,1,0:T(8,128)} %gather_fusion, f32[64,3]{1,0:T(8,128)S(1)} %copy.98, f32[64,3]{1,0:T(8,128)S(1)} %copy.99, bf16[64,3,33,384]{3,2,1,0:T(8,128)(2,1)} %gather_fusion.1, bf16[64,3,128,384]{3,2,0,1:T(8,128)(2,1)} %bitcast.52), kind=kOutput, calls=%fused_computation.12.clone.1 | convolution fusion | flops 626638848 | bytes 27526656 | tf_op jit(solution)/shard_map/while/body/eval_jaxpr/gcbm,gcjm->gcbj/dot_general | solution.py:89
  375.1 1.9 fusion.51
  378.1 3.9 gather_fusion.1
  382.0 2.7 gather_fusion
  384.8 8.4 %broadcast_in_dim.41 = bf16[64,3,128,385]{3,2,0,1:T(8,128)(2,1)} broadcast(bf16[64,3,385]{2,0,1:T(8,128)(2,1)S(1)} %concatenate.17), dimensions={0,1,3} | broadcast | bytes 19071360 | tf_op jit(solution)/shard_map/while/body/eval_jaxpr/broadcast_in_dim | solution.py:14
  393.3 35.9 %reshape.206 = bf16[64,3,49280]{2,0,1:T(8,128)(2,1)} reshape(bf16[64,3,128,385]{3,2,0,1:T(8,128)(2,1)} %broadcast_in_dim.41) | data formatting | bytes 37847040 | tf_op jit(solution)/shard_map/while/body/eval_jaxpr/reshape | solution.py:16
  429.2 6.4 %slice-done = bf16[64,3,49152]{2,0,1:T(8,128)(2,1)S(1)} async-done(((bf16[64,3,49280]{2,0,1:T(8,128)(2,1)}), bf16[64,3,49152]{2,0,1:T(8,128)(2,1)S(1)}, s32[]{:S(2)}) %slice-start) | async-done | bytes 18874392 | tf_op jit(solution)/shard_map/while/body/eval_jaxpr/slice | solution.py:17
  435.6 7.0 %copy.100 = bf16[24,8,128,384]{3,2,1,0:T(8,128)(2,1)} copy(bf16[24,8,128,384]{3,1,2,0:T(8,128)(2,1)S(1)} %bitcast.51) | data formatting | bytes 37748736 | tf_op jit(solution)/shard_map/while
  442.8 14.0 %multiply_reduce_fusion.6 = bf16[64,33,128]{2,1,0:T(8,128)(2,1)S(1)} fusion(f32[64,3,33,128]{3,2,1,0:T(8,128)} %gather_fusion, f32[64,3]{1,0:T(8,128)S(1)} %copy.98, f32[64,3]{1,0:T(8,128)S(1)} %copy.99, bf16[64,3,33,384]{3,2,1,0:T(8,128)(2,1)} %gather_fusion.1, bf16[64,3,128,384]{3,2,0,1:T(8,128)(2,1)} %bitcast.52), kind=kOutput, calls=%fused_computation.12.clone.1 | convolution fusion | flops 626638848 | bytes 27526656 | tf_op jit(solution)/shard_map/while/body/eval_jaxpr/gcbm,gcjm->gcbj/dot_general | solution.py:89
  457.2 1.9 fusion.51
  460.1 3.9 gather_fusion.1
  464.0 2.7 gather_fusion
  466.8 8.4 %broadcast_in_dim.41 = bf16[64,3,128,385]{3,2,0,1:T(8,128)(2,1)} broadcast(bf16[64,3,385]{2,0,1:T(8,128)(2,1)S(1)} %concatenate.17), dimensions={0,1,3} | broadcast | bytes 19071360 | tf_op jit(solution)/shard_map/while/body/eval_jaxpr/broadcast_in_dim | solution.py:14
  475.3 35.9 %reshape.206 = bf16[64,3,49280]{2,0,1:T(8,128)(2,1)} reshape(bf16[64,3,128,385]{3,2,0,1:T(8,128)(2,1)} %broadcast_in_dim.41) | data formatting | bytes 37847040 | tf_op jit(solution)/shard_map/while/body/eval_jaxpr/reshape | solution.py:16
  511.2 6.4 %slice-done = bf16[64,3,49152]{2,0,1:T(8,128)(2,1)S(1)} async-done(((bf16[64,3,49280]{2,0,1:T(8,128)(2,1)}), bf16[64,3,49152]{2,0,1:T(8,128)(2,1)S(1)}, s32[]{:S(2)}) %slice-start) | async-done | bytes 18874392 | tf_op jit(solution)/shard_map/while/body/eval_jaxpr/slice | solution.py:17
  517.6 7.0 %copy.100 = bf16[24,8,128,384]{3,2,1,0:T(8,128)(2,1)} copy(bf16[24,8,128,384]{3,1,2,0:T(8,128)(2,1)S(1)} %bitcast.51) | data formatting | bytes 37748736 | tf_op jit(solution)/shard_map/while
  524.8 14.0 %multiply_reduce_fusion.6 = bf16[64,33,128]{2,1,0:T(8,128)(2,1)S(1)} fusion(f32[64,3,33,128]{3,2,1,0:T(8,128)} %gather_fusion, f32[64,3]{1,0:T(8,128)S(1)} %copy.98, f32[64,3]{1,0:T(8,128)S(1)} %copy.99, bf16[64,3,33,384]{3,2,1,0:T(8,128)(2,1)} %gather_fusion.1, bf16[64,3,128,384]{3,2,0,1:T(8,128)(2,1)} %bitcast.52), kind=kOutput, calls=%fused_computation.12.clone.1 | convolution fusion | flops 626638848 | bytes 27526656 | tf_op jit(solution)/shard_map/while/body/eval_jaxpr/gcbm,gcjm->gcbj/dot_general | solution.py:89
  539.2 1.9 fusion.51
  542.1 7.1 %reshape.139 = bf16[128,3,4096]{2,1,0:T(4,128)(2,1)} reshape(bf16[6,64,4096]{2,1,0:T(8,128)(2,1)} %get-tuple-element.47) | data formatting | bytes 6291456 | tf_op jit(solution)/shard_map/reshape | solution.py:114
  549.2 5.8 all-to-all-start.2
  555.1 52.6 %all-to-all-done.2 = bf16[128,3,4096]{2,1,0:T(4,128)(2,1)} async-done(((bf16[128,3,4096]{2,1,0:T(4,128)(2,1)}), bf16[128,3,4096]{2,1,0:T(4,128)(2,1)}, u32[]{:S(2)}, u32[]{:S(2)}) %all-to-all-start.2) | async-done | bytes 3145760 | tf_op jit(solution)/shard_map/all_to_all | solution.py:113
  607.7 6.0 reshape.140
  613.7 3.1 gather_fusion.2
  616.8 4.3 reshape.142
  621.1 4.0 reduce_sum.49
  (124 shorter events, 20.1 us)
Async XLA Ops:
  0.0 34.2 %copy-start = (bf16[8,3,4480]{2,0,1:T(8,128)(2,1)S(1)}, bf16[8,3,4480]{2,0,1:T(8,128)(2,1)}, u32[]{:S(2)}) copy-start(bf16[8,3,4480]{2,0,1:T(8,128)(2,1)} %param.8) | copy-start | bytes 645124
  5.2 29.1 %copy-start.1 = (s32[240,1]{0,1:T(1,128)}, s32[240,1]{0,1:T(1,128)S(1)}, u32[]{:S(2)}) copy-start(s32[240,1]{0,1:T(1,128)S(1)} %compare_select_fusion.1) | copy-start | bytes 2884
  7.1 22.3 %all-to-all-start = ((s32[128,3,5]{2,1,0:T(4,128)}), s32[128,3,5]{2,1,0:T(4,128)S(1)}, u32[]{:S(2)}, u32[]{:S(2)}) async-start(s32[128,3,5]{2,1,0:T(4,128)} %reshape.191), calls=%async_computation | async-start | bytes 524288 | tf_op jit(solution)/shard_map/all_to_all | solution.py:64
  29.4 19.7 %all-to-all-start.1 = ((bf16[128,3,600]{2,1,0:T(4,128)(2,1)}), bf16[128,3,600]{2,1,0:T(4,128)(2,1)S(1)}, u32[]{:S(2)}, u32[]{:S(2)}) async-start(bf16[128,3,600]{2,1,0:T(4,128)(2,1)} %reshape.137), calls=%async_computation.1 | async-start | bytes 1310720 | tf_op jit(solution)/shard_map/all_to_all | solution.py:57
  101.0 6.4 %slice-start = ((bf16[64,3,49280]{2,0,1:T(8,128)(2,1)}), bf16[64,3,49152]{2,0,1:T(8,128)(2,1)S(1)}, s32[]{:S(2)}) async-start(bf16[64,3,49280]{2,0,1:T(8,128)(2,1)} %reshape.206), calls=%async_computation.3 | async-start | bytes 37748736 | tf_op jit(solution)/shard_map/while/body/eval_jaxpr/slice | solution.py:17
  183.1 6.4 %slice-start = ((bf16[64,3,49280]{2,0,1:T(8,128)(2,1)}), bf16[64,3,49152]{2,0,1:T(8,128)(2,1)S(1)}, s32[]{:S(2)}) async-start(bf16[64,3,49280]{2,0,1:T(8,128)(2,1)} %reshape.206), calls=%async_computation.3 | async-start | bytes 37748736 | tf_op jit(solution)/shard_map/while/body/eval_jaxpr/slice | solution.py:17
  265.1 6.4 %slice-start = ((bf16[64,3,49280]{2,0,1:T(8,128)(2,1)}), bf16[64,3,49152]{2,0,1:T(8,128)(2,1)S(1)}, s32[]{:S(2)}) async-start(bf16[64,3,49280]{2,0,1:T(8,128)(2,1)} %reshape.206), calls=%async_computation.3 | async-start | bytes 37748736 | tf_op jit(solution)/shard_map/while/body/eval_jaxpr/slice | solution.py:17
  347.2 6.4 %slice-start = ((bf16[64,3,49280]{2,0,1:T(8,128)(2,1)}), bf16[64,3,49152]{2,0,1:T(8,128)(2,1)S(1)}, s32[]{:S(2)}) async-start(bf16[64,3,49280]{2,0,1:T(8,128)(2,1)} %reshape.206), calls=%async_computation.3 | async-start | bytes 37748736 | tf_op jit(solution)/shard_map/while/body/eval_jaxpr/slice | solution.py:17
  429.2 6.4 %slice-start = ((bf16[64,3,49280]{2,0,1:T(8,128)(2,1)}), bf16[64,3,49152]{2,0,1:T(8,128)(2,1)S(1)}, s32[]{:S(2)}) async-start(bf16[64,3,49280]{2,0,1:T(8,128)(2,1)} %reshape.206), calls=%async_computation.3 | async-start | bytes 37748736 | tf_op jit(solution)/shard_map/while/body/eval_jaxpr/slice | solution.py:17
  511.2 6.4 %slice-start = ((bf16[64,3,49280]{2,0,1:T(8,128)(2,1)}), bf16[64,3,49152]{2,0,1:T(8,128)(2,1)S(1)}, s32[]{:S(2)}) async-start(bf16[64,3,49280]{2,0,1:T(8,128)(2,1)} %reshape.206), calls=%async_computation.3 | async-start | bytes 37748736 | tf_op jit(solution)/shard_map/while/body/eval_jaxpr/slice | solution.py:17
  549.2 5.9 copy-start.2
  549.2 58.5 %all-to-all-start.2 = ((bf16[128,3,4096]{2,1,0:T(4,128)(2,1)}), bf16[128,3,4096]{2,1,0:T(4,128)(2,1)}, u32[]{:S(2)}, u32[]{:S(2)}) async-start(bf16[128,3,4096]{2,1,0:T(4,128)(2,1)} %reshape.139), calls=%async_computation.2 | async-start | bytes 8388608 | tf_op jit(solution)/shard_map/all_to_all | solution.py:113
where the time goes:
time: 632 us; the launch traced here: 626 us
  local copies, waits for them, and re-layouts  427 us (68%)
  matrix products  95.9 us (15%)
  waiting for transfers between devices  72.6 us (11%)
  starting transfers between devices  22.1 us (3%)
  other arithmetic  7.51 us (1%)
    reshape x6, local copies, waits for them, and re-layouts, toeplitz_rows(): repeated = jnp.broadcast_to(padded[:, :, None, :], (group_size, channels,...  216 us
    dot_general x6, matrix products, correlate(): jnp.einsum('gcbm,gcjm->gcbj', windows, toeplitz, preferred_element_type=j...  83.8 us
    all_to_all x1, waiting for transfers between devices, on_device(): lax.all_to_all(outgoing.reshape(devices, capacity, lag_count), ('sta', 't...  52.6 us
    broadcast_in_dim x6, local copies, waits for them, and re-layouts, toeplitz_rows(): jnp.broadcast_to(padded[:, :, None, :], (group_size, channels, 128, frame...  50.7 us
    while x6, local copies, waits for them, and re-layouts  42.3 us
    slice x12, local copies, waits for them, and re-layouts, toeplitz_rows(): repeated[:, :, :128 * frame_len]  38.2 us
    gather x6, local copies, waits for them, and re-layouts, correlate(): windows = frames[stations]  23.5 us
    gather x6, local copies, waits for them, and re-layouts, correlate(): energy[stations]  16 us
  transfers between devices with their start and end apart: 3, of which 3 were waited for; matrix products, arithmetic and copies ran while one was open for 1% of the time, Pallas kernels for 0%

commit v1 on v0

v1 whole, which is shorter than its diff:
```python
import functools

import jax
import jax.numpy as jnp
from jax import lax
from jax.experimental import pallas as pl
from jax.experimental.pallas import tpu as pltpu
from jax.sharding import PartitionSpec as P

EPS = 1e-06
CAP = 3
SIDE = 4
UNROLL = 8
INFO = 8


def shifted(axis, step):
    if axis == "x":
        return [(x * SIDE + z, ((x + step) % SIDE) * SIDE + z) for x in range(SIDE) for z in range(SIDE)]
    return [(x * SIDE + z, x * SIDE + (z + step) % SIDE) for x in range(SIDE) for z in range(SIDE)]


def ring(block, axis):
    behind = lax.ppermute(block, "sta", shifted(axis, 1))
    ahead = lax.ppermute(block, "sta", shifted(axis, -1))
    half = block.shape[0] // 2
    far_a = lax.ppermute(behind[:half], "sta", shifted(axis, 1))
    far_b = lax.ppermute(ahead[half:], "sta", shifted(axis, -1))
    return behind, ahead, far_a, far_b


def pick_kernel(picks_per_source, taps, counts, info, power, inbox, *refs):
    piece_count = 10
    pieces = refs[:piece_count]
    out, records, frames, energy, total, shapes, wide, sums, sem = refs[piece_count:]
    copies = []
    base = 0
    for number, piece in enumerate(pieces):
        size = piece.shape[0]
        copies.append((base, size, pltpu.make_async_copy(piece, records.at[pl.ds(base, size)], sem.at[number])))
        base += size
    for _, _, copy in copies:
        copy.start()

    lanes = lax.broadcasted_iota(jnp.int32, (inbox.shape[0], 128), 1)
    for k in range(inbox.shape[1] // 128):
        block = inbox[:, k * 128 : k * 128 + 128].astype(jnp.float32)
        if k == 0:
            block = jnp.where(lanes < INFO, 0.0, block)
        shapes[pl.ds(k, inbox.shape[0], stride=8), :] = block
    total[...] = jnp.zeros_like(total)

    row = lax.broadcasted_iota(jnp.int32, (256, 384), 0)
    column = lax.broadcasted_iota(jnp.int32, (256, 384), 1)
    reach = (column // 128) * 128 + row % 128 - column % 128
    band = jnp.where((reach >= 0) & (reach < taps), 1.0, 0.0).astype(jnp.bfloat16)
    group = sums.shape[0] // 112

    def prepare(step, carry):
        x = records[pl.ds(step * group, group)].reshape(group * 112, 128).astype(jnp.float32)
        wide[...] = x
        square = x * x
        high = square.astype(jnp.bfloat16)
        low = (square - high.astype(jnp.float32)).astype(jnp.bfloat16)
        sums[...] = jnp.dot(jnp.concatenate([high, low], axis=1), band, preferred_element_type=jnp.float32)
        for s in range(group):
            for c in range(3):
                at = s * 112 + c * 35
                slot = (step * group + s) * 3 + c
                energy[slot] = (
                    sums[at : at + 40, 0:128] + sums[at + 1 : at + 41, 128:256] + sums[at + 2 : at + 42, 256:384]
                )
                for q in range(3):
                    frames[slot, 0:40, q * 128 : q * 128 + 128] = wide[at + q : at + q + 40, :].astype(jnp.bfloat16)
        return carry

    for first, size, copy in copies:
        copy.wait()
        lax.fori_loop(first // group, (first + size) // group, prepare, 0)

    across = lax.broadcasted_iota(jnp.int32, (128, 128), 1)
    below = across <= lax.broadcasted_iota(jnp.int32, (128, 128), 0)
    nothing = jnp.zeros((128, 128), jnp.bfloat16)
    lag = lax.broadcasted_iota(jnp.int32, (32, 128), 1)

    def spread(line):
        block = jnp.broadcast_to(line, (128, 128))
        return pltpu.roll(block, 1, 1, stride=1, stride_axis=0).astype(jnp.bfloat16)

    def one_pick(i):
        station, shift, target = info[INFO * i], info[INFO * i + 1], info[INFO * i + 2]
        trace = None
        lines = shapes[pl.ds(pl.multiple_of(8 * i, 8), 8), :]
        for c in range(3):
            late = spread(lines[2 * c : 2 * c + 1])
            early = spread(lines[2 * c + 1 : 2 * c + 2])
            toeplitz = jnp.concatenate(
                [jnp.where(below, early, nothing), jnp.where(below, late, early), jnp.where(below, nothing, late)],
                axis=0,
            )
            number = jnp.dot(frames[3 * station + c], toeplitz, preferred_element_type=jnp.float32)[:40]
            level = lax.rsqrt(power[4 * i + c] * energy[3 * station + c] + EPS)
            scaled = number * level * info[INFO * i + 3 + c].astype(jnp.float32)
            trace = scaled if trace is None else trace + scaled
        trace = trace.astype(jnp.bfloat16).astype(jnp.float32)
        turned = pltpu.roll(trace, 128 - shift, 1)
        following = pltpu.roll(turned, 39, 0)
        total[target] += jnp.where(lag < 128 - shift, turned[:32], following[:32])

    for source in range(out.shape[0] // 24):
        def several(step, carry):
            for u in range(UNROLL):
                one_pick(source * picks_per_source + step * UNROLL + u)
            return carry

        lax.fori_loop(0, (counts[source] + UNROLL - 1) // UNROLL, several, 0)
    out[...] = total[...].astype(out.dtype)


def stack_kernel(parts, out, total):
    rows = out.shape[0]
    summed = parts[0].astype(jnp.float32)
    for p in range(1, parts.shape[0]):
        summed = summed + parts[p].astype(jnp.float32)
    cube = summed.reshape(rows, 32, 128)
    square = jnp.sum(jnp.sum(cube * cube, axis=2, keepdims=True), axis=1, keepdims=True)
    level = jnp.sqrt(square / (32 * 128) + EPS)
    total[...] = (cube / level).reshape(rows * 32, 128)
    for b in range(32):
        out[:, b * 128 : b * 128 + 128] = total[pl.ds(b, rows, stride=32), :]


def on_device(records, templates, pick_owner, pick_local, moveout, channel_mask):
    own_templates, pick_count, channels, taps = templates.shape
    columns = lax.axis_size("tpl")
    lines = lax.axis_size("sta")
    rows = own_templates * pick_count
    per_source = CAP * lines
    slots = columns * per_source
    stations = lines * records.shape[0]
    vmem, smem = pl.BlockSpec(memory_space=pltpu.VMEM), pl.BlockSpec(memory_space=pltpu.SMEM)

    pieces = records.reshape(records.shape[0], 105, 128)
    pieces = jnp.pad(pieces, ((0, 0), (0, 7), (0, 0)))
    half = records.shape[0] // 2
    by_x = jnp.concatenate((pieces[:half],) + ring(pieces[:half], "x"))
    by_z = jnp.concatenate((pieces[half:],) + ring(pieces[half:], "z"))
    gathered = (by_x,) + ring(by_x, "z") + (by_z,) + ring(by_z, "x")

    here = lax.axis_index("sta")
    owner = pick_owner.reshape(rows)
    line, column = owner // columns, owner % columns
    ahead_x = (line // SIDE - here // SIDE) % SIDE
    ahead_z = (line % SIDE - here % SIDE) % SIDE
    order_x = jnp.where(ahead_x == 3, 1, jnp.where(ahead_x == 0, 0, ahead_x + 1))
    order_z = jnp.where(ahead_z == 3, 1, jnp.where(ahead_z == 0, 0, ahead_z + 1))
    local = pick_local.reshape(rows)
    station = jnp.where(
        local < half,
        16 * order_z + 4 * order_x + local,
        64 + 16 * order_x + 4 * order_z + local - half,
    )
    onehot = (column[:, None] == jnp.arange(columns, dtype=jnp.int32)[None, :]).astype(jnp.int32)
    before = jnp.cumsum(onehot, axis=0) - onehot
    position = column * per_source + jnp.sum(before * onehot, axis=1)
    target = jnp.arange(rows, dtype=jnp.int32) // pick_count
    details = jnp.concatenate(
        [
            station[:, None],
            moveout.reshape(rows, 1),
            target[:, None],
            channel_mask.reshape(rows, channels),
            jnp.ones((rows, 1), jnp.int32),
        ],
        axis=1,
    ).astype(jnp.bfloat16)
    front = jnp.pad(details, ((0, 0), (0, 56 - details.shape[1])))[:, None, :]
    front = jnp.pad(front, ((0, 0), (0, channels - 1), (0, 0)))
    sent = jnp.concatenate([front, templates.reshape(rows, channels, taps)[:, :, ::-1]], axis=2)
    place = (position[None, :] == jnp.arange(slots, dtype=jnp.int32)[:, None]).astype(jnp.bfloat16)
    outbox = jnp.dot(place, sent.reshape(rows, channels * 256), preferred_element_type=jnp.float32)
    inbox = lax.all_to_all(
        outbox.astype(jnp.bfloat16).reshape(columns, per_source, channels * 256),
        "tpl",
        split_axis=0,
        concat_axis=0,
        tiled=True,
    )
    marks = inbox[:, :, :INFO].astype(jnp.int32)
    counts = jnp.sum(marks[:, :, 6], axis=1)
    offset = own_templates * jnp.arange(columns, dtype=jnp.int32)[:, None]
    marks = marks.at[:, :, 2].add(offset).reshape(slots * INFO)
    inbox = inbox.reshape(slots, channels * 256)
    wide = inbox.reshape(slots, channels, 256)[:, :, 56:].astype(jnp.float32)
    power = jnp.pad(jnp.sum(wide * wide, axis=2), ((0, 0), (0, 1))).reshape(slots * 4)

    total_rows = columns * own_templates
    partial = pl.pallas_call(
        functools.partial(pick_kernel, per_source, taps),
        out_shape=jax.ShapeDtypeStruct((total_rows, 32, 128), jnp.bfloat16),
        in_specs=[smem, smem, smem, vmem] + [pl.BlockSpec(memory_space=pl.ANY)] * len(gathered),
        out_specs=vmem,
        scratch_shapes=[
            pltpu.VMEM((stations, 112, 128), jnp.bfloat16),
            pltpu.VMEM((stations * 3, 48, 384), jnp.bfloat16),
            pltpu.VMEM((stations * 3, 40, 128), jnp.float32),
            pltpu.VMEM((total_rows, 32, 128), jnp.float32),
            pltpu.VMEM((slots * 8, 128), jnp.float32),
            pltpu.VMEM((8 * 112, 128), jnp.float32),
            pltpu.VMEM((8 * 112, 384), jnp.float32),
            pltpu.SemaphoreType.DMA((len(gathered),)),
        ],
        compiler_params=pltpu.CompilerParams(vmem_limit_bytes=56 * 2**20),
    )(counts, marks, power, inbox, *gathered)

    returned = lax.all_to_all(
        partial.reshape(columns, own_templates * 32, 128), "tpl", split_axis=0, concat_axis=0, tiled=True
    )
    return pl.pallas_call(
        stack_kernel,
        out_shape=jax.ShapeDtypeStruct((own_templates, 4096), jnp.float32),
        in_specs=[vmem],
        out_specs=vmem,
        scratch_shapes=[pltpu.VMEM((own_templates * 32, 128), jnp.float32)],
        compiler_params=pltpu.CompilerParams(vmem_limit_bytes=32 * 2**20),
    )(returned)


def solution(mesh):
    return jax.shard_map(
        on_device,
        mesh=mesh,
        in_specs=(
            P(("sta", "tpl"), None, None),
            P(("sta", "tpl"), None, None, None),
            P(("sta", "tpl"), None),
            P(("sta", "tpl"), None),
            P(("sta", "tpl"), None),
            P(("sta", "tpl"), None, None),
        ),
        out_specs=P(("sta", "tpl"), None),
        check_vma=False,
    )
```

time: 632 us -> 126 us (0.20); the launches traced: 626 us -> 127 us
  local copies, waits for them, and re-layouts: 427 us -> 16.2 us
  matrix products: 95.9 us -> 1.18 us
  waiting for transfers between devices: 72.6 us -> 9.28 us
  Pallas kernels: 0 us -> 36.1 us
  blocking collectives: 0 us -> 32.8 us
    reshape x16 -> x9, local copies, waits for them, and re-layouts: 232 us -> 2.37 us  [the longest x1 0.73 us: on_device(): jnp.pad(jnp.sum(wide * wide, axis=2), ((0, 0), (0, 1))).reshape(slots * 4)]
    dot_general x13 -> x1, matrix products: 95.9 us -> 1.18 us  [on_device(): jnp.dot(place, sent.reshape(rows, channels * 256), preferred_element_type...]
    all_to_all x3 -> x1, waiting for transfers between devices: 72.6 us -> 0.01 us  [on_device(): lax.all_to_all(outbox.astype(jnp.bfloat16).reshape(columns, per_source, c...]
    broadcast_in_dim x12 -> x1, local copies, waits for them, and re-layouts: 52 us -> 0.01 us  [on_device(): front = jnp.pad(details, ((0, 0), (0, 56 - details.shape[1])))[:, None, :]]
    gather x13 -> x0, local copies, waits for them, and re-layouts: 42.5 us -> none  [the longest x6 23.5 us: correlate(): windows = frames[stations]]
    while x6 -> x0, local copies, waits for them, and re-layouts: 42.3 us -> none
    slice x19 -> x9, local copies, waits for them, and re-layouts: 40.1 us -> 3.02 us  [the longest x4 1.5 us: ring(): far_a = lax.ppermute(behind[:half], 'sta', shifted(axis, 1))]
    pallas_call x0 -> x2, Pallas kernels: none -> 36.1 us  [the longest x1 34.8 us: on_device(): pl.pallas_call(functools.partial(pick_kernel, per_source, taps), out_shap...]
  transfers between devices with their start and end apart: 3 -> 17, of which waited for: 3 -> 3; matrix products, arithmetic and copies ran while one was open for 1% -> 15% of each run, Pallas kernels for 0% -> 0%
where the time goes in v1:
time: 126 us; the launch traced here: 127 us
  Pallas kernels  36.1 us (29%)
  blocking collectives  32.8 us (26%)
  starting transfers between devices  28.1 us (22%)
  local copies, waits for them, and re-layouts  16.2 us (13%)
  waiting for transfers between devices  9.28 us (7%)
  other arithmetic  3.14 us (2%)
    pallas_call x1, Pallas kernels, on_device(): pl.pallas_call(functools.partial(pick_kernel, per_source, taps), out_shap...  34.8 us
    all_to_all x1, blocking collectives, on_device(): lax.all_to_all(partial.reshape(columns, own_templates * 32, 128), 'tpl',...  32.8 us
    ppermute x4, starting transfers between devices, ring(): far_b = lax.ppermute(ahead[half:], 'sta', shifted(axis, -1))  10.9 us
    ppermute x4, starting transfers between devices, ring(): ahead = lax.ppermute(block, 'sta', shifted(axis, -1))  10.6 us
    unnamed x33, local copies, waits for them, and re-layouts  7.73 us
    all_to_all x1, starting transfers between devices, on_device(): lax.all_to_all(outbox.astype(jnp.bfloat16).reshape(columns, per_source, c...  5.7 us
    ppermute x4, waiting for transfers between devices, ring(): ahead = lax.ppermute(block, 'sta', shifted(axis, -1))  5.65 us
    ppermute x4, waiting for transfers between devices, ring(): far_a = lax.ppermute(behind[:half], 'sta', shifted(axis, 1))  3.6 us
  transfers between devices with their start and end apart: 17, of which 3 were waited for; matrix products, arithmetic and copies ran while one was open for 15% of the time, Pallas kernels for 0%

profile of v1, /device:TPU:1, one launch (start us, length us, event | category | flops | bytes accessed | tf_op | source)
XLA Modules:
  0.0 127.1 jit_solution(5634174137841245211)
XLA Ops:
  0.0 1.1 copy.17
  1.1 0.2 reshape.467
  1.3 0.7 pad_slice_fusion
  2.1 4.6 %collective-permute-start.9 = (bf16[4,112,128]{2,1,0:T(8,128)(2,1)S(1)}, bf16[4,112,128]{2,1,0:T(8,128)(2,1)S(1)}, u32[]{:S(2)}, u32[]{:S(2)}) collective-permute-start(bf16[4,112,128]{2,1,0:T(8,128)(2,1)S(1)} %get-tuple-element.17), channel_id=1, source_target_pairs={{0,24},{8,0},{16,8},{24,16},{32,56},{40,32},{48,40},{56,48},{64,88... | collective-permute-start | bytes 344072 | tf_op jit(solution)/shard_map/ppermute | solution.py:25
  6.6 0.0 collective-permute-start.8
  6.7 2.5 %collective-permute-start.1 = (bf16[4,112,128]{2,1,0:T(8,128)(2,1)S(1)}, bf16[4,112,128]{2,1,0:T(8,128)(2,1)S(1)}, u32[]{:S(2)}, u32[]{:S(2)}) collective-permute-start(bf16[4,112,128]{2,1,0:T(8,128)(2,1)S(1)} %get-tuple-element.20), channel_id=1, source_target_pairs={{0,96},{8,104},{16,112},{24,120},{32,0},{40,8},{48,16},{56,24},{64... | collective-permute-start | bytes 344072 | tf_op jit(solution)/shard_map/ppermute | solution.py:25
  9.1 0.0 collective-permute-start
  9.1 0.1 copy.9
  9.2 0.1 reshape.454
  9.3 0.1 reshape.458
  9.5 0.1 copy.12
  9.5 0.1 reshape.459
  9.7 0.1 copy.13
  9.8 0.1 reshape.460
  9.9 0.6 reduce-window.6
  10.5 0.2 slice_reduce_fusion.1
  10.8 0.1 add_bitcast_fusion
  10.9 0.1 copy.10
  11.0 0.1 reshape.457
  11.2 0.1 copy.18
  11.3 0.1 copy.14
  11.4 0.2 reshape.461
  11.7 2.2 %reverse = bf16[240,3,256]{2,0,1:T(8,128)(2,1)S(1)} reverse(bf16[240,3,256]{2,0,1:T(8,128)(2,1)S(1)} %bitcast.21), dimensions={2} | reverse | bytes 737280
  13.9 0.2 slice.119
  14.1 0.2 fusion.1
  14.2 0.2 copy.16
  14.4 1.2 convolution_convert_fusion
  15.6 5.7 %all-to-all-start = ((bf16[8,48,768]{2,1,0:T(8,128)(2,1)}), bf16[8,48,768]{2,1,0:T(8,128)(2,1)S(1)}, u32[]{:S(2)}, u32[]{:S(2)}) async-start(bf16[8,48,768]{2,1,0:T(8,128)(2,1)} %bitcast.5), calls=%async_computation | async-start | bytes 1179648 | tf_op jit(solution)/shard_map/all_to_all | solution.py:182
  21.3 0.0 collective-permute-done.9
  21.3 3.0 %collective-permute-start.11 = (bf16[2,112,128]{2,1,0:T(8,128)(2,1)S(1)}, bf16[2,112,128]{2,1,0:T(8,128)(2,1)S(1)}, u32[]{:S(2)}, u32[]{:S(2)}) collective-permute-start(bf16[2,112,128]{2,1,0:T(8,128)(2,1)S(1)} %slice.100), channel_id=1, source_target_pairs={{0,24},{8,0},{16,8},{24,16},{32,56},{40,32},{48,40},{56,48},{64,88... | collective-permute-start | bytes 172040 | tf_op jit(solution)/shard_map/ppermute | solution.py:28
  24.3 0.1 collective-permute-start.10
  24.4 0.0 collective-permute-done.1
  24.4 3.0 %collective-permute-start.3 = (bf16[2,112,128]{2,1,0:T(8,128)(2,1)S(1)}, bf16[2,112,128]{2,1,0:T(8,128)(2,1)S(1)}, u32[]{:S(2)}, u32[]{:S(2)}) collective-permute-start(bf16[2,112,128]{2,1,0:T(8,128)(2,1)S(1)} %slice.96), channel_id=1, source_target_pairs={{0,96},{8,104},{16,112},{24,120},{32,0},{40,8},{48,16},{56,24},{64... | collective-permute-start | bytes 172040 | tf_op jit(solution)/shard_map/ppermute | solution.py:28
  27.5 0.0 collective-permute-done
  27.5 0.1 collective-permute-start.2
  27.6 0.6 constant_dynamic-update-slice_fusion.8
  28.2 0.6 constant_dynamic-update-slice_fusion.7
  28.8 0.6 constant_dynamic-update-slice_fusion.3
  29.5 0.7 constant_dynamic-update-slice_fusion.2
  30.1 1.8 %collective-permute-done.2 = bf16[2,112,128]{2,1,0:T(8,128)(2,1)S(1)} collective-permute-done((bf16[2,112,128]{2,1,0:T(8,128)(2,1)S(1)}, bf16[2,112,128]{2,1,0:T(8,128)(2,1)S(1)}, u32[]{:S(2)}, u32[]{:S(2)}) %collective-permute-start.2) | collective-permute-done | bytes 57376 | tf_op jit(solution)/shard_map/ppermute | solution.py:27
  32.0 0.6 constant_dynamic-update-slice_fusion.1
  32.6 0.6 constant_dynamic-update-slice_fusion.refs_0_
  33.2 2.8 %collective-permute-start.5 = (bf16[16,112,128]{2,1,0:T(8,128)(2,1)}, bf16[16,112,128]{2,1,0:T(8,128)(2,1)S(1)}, u32[]{:S(2)}, u32[]{:S(2)}) collective-permute-start(bf16[16,112,128]{2,1,0:T(8,128)(2,1)} %constant_dynamic-update-slice_fusion.refs_0_), channel_id=1, source_target_pairs={{0,24},{8,0},{16,8},{24,16},{32,56},{40,32},{48,40},{56,48},{64,88... | collective-permute-start | bytes 1376264 | tf_op jit(solution)/shard_map/ppermute | solution.py:25
  36.0 0.6 constant_dynamic-update-slice_fusion.6
  36.6 0.6 constant_dynamic-update-slice_fusion.5.refs_5_
  37.3 0.7 collective-permute-start.13
  38.0 0.7 collective-permute-start.12
  38.8 5.6 %collective-permute-done.5.refs_2_ = bf16[16,112,128]{2,1,0:T(8,128)(2,1)S(1)} collective-permute-done((bf16[16,112,128]{2,1,0:T(8,128)(2,1)}, bf16[16,112,128]{2,1,0:T(8,128)(2,1)S(1)}, u32[]{:S(2)}, u32[]{:S(2)}) %collective-permute-start.5) | collective-permute-done | bytes 458784 | tf_op jit(solution)/shard_map/ppermute | solution.py:25
  44.4 3.4 %collective-permute-start.7 = (bf16[8,112,128]{2,1,0:T(8,128)(2,1)S(1)}, bf16[8,112,128]{2,1,0:T(8,128)(2,1)}, u32[]{:S(2)}, u32[]{:S(2)}) collective-permute-start(bf16[8,112,128]{2,1,0:T(8,128)(2,1)S(1)} %slice.98), channel_id=1, source_target_pairs={{0,24},{8,0},{16,8},{24,16},{32,56},{40,32},{48,40},{56,48},{64,88... | collective-permute-start | bytes 688136 | tf_op jit(solution)/shard_map/ppermute | solution.py:28
  47.8 0.7 slice.97
  48.6 0.7 slice.102
  49.3 1.5 %collective-permute-start.15 = (bf16[8,112,128]{2,1,0:T(8,128)(2,1)}, bf16[8,112,128]{2,1,0:T(8,128)(2,1)}, u32[]{:S(2)}, u32[]{:S(2)}) collective-permute-start(bf16[8,112,128]{2,1,0:T(8,128)(2,1)} %slice.102), channel_id=1, source_target_pairs={{0,96},{8,104},{16,112},{24,120},{32,0},{40,8},{48,16},{56,24},{64... | collective-permute-start | bytes 688136 | tf_op jit(solution)/shard_map/ppermute | solution.py:28
  50.8 0.8 slice.101
  51.5 0.0 collective-permute-start.14
  51.5 0.9 slice_add_fusion
  52.5 0.9 scatter-add.4
  53.4 0.7 reshape.464.info
  54.1 0.3 reshape_reshape.3
  54.4 1.2 multiply_reduce_fusion
  55.7 0.7 reshape.465.power
  56.4 1.8 %collective-permute-done.14.refs_8_ = bf16[8,112,128]{2,1,0:T(8,128)(2,1)} collective-permute-done((bf16[8,112,128]{2,1,0:T(8,128)(2,1)}, bf16[8,112,128]{2,1,0:T(8,128)(2,1)}, u32[]{:S(2)}, u32[]{:S(2)}) %collective-permute-start.14) | collective-permute-done | bytes 229408 | tf_op jit(solution)/shard_map/ppermute | solution.py:27
  58.2 34.8 %shard_map.64 = bf16[192,32,128]{2,1,0:T(8,128)(2,1)} custom-call(s32[8]{0:T(128)} %get-tuple-element.22.counts, s32[3072]{0:T(1024)} %reshape.464.info, f32[1536]{0:T(1024)} %reshape.465.power, bf16[384,768]{1,0:T(8,128)(2,1)} %bitcast.19, bf16[16,112,128]{2,1,0:T(8,128)(2,1)} %constant_dynamic-update-slice_fusion.refs_0_, bf16[16,112,128]{2,1,0:T(8,128)(2,1)} %copy-done.2, ...), custom_call_target="tpu_custom_call" | custom-call | tf_op jit(solution)/shard_map/pallas_call | solution.py:198
  93.1 32.8 %all_to_all.10.parts = bf16[8,768,128]{2,1,0:T(8,128)(2,1)S(1)} all-to-all(bf16[8,768,128]{2,1,0:T(8,128)(2,1)} %bitcast.18), channel_id=1, replica_groups=mesh['sta'=16,'tpl'=8] {'tpl'}, dimensions={0} | all-to-all | bytes 3145728 | tf_op jit(solution)/shard_map/all_to_all | solution.py:216
  125.8 1.3 %shard_map.65 = f32[24,4096]{1,0:T(8,128)} custom-call(bf16[8,768,128]{2,1,0:T(8,128)(2,1)S(1)} %all_to_all.10.parts), custom_call_target="tpu_custom_call" | custom-call | tf_op jit(solution)/shard_map/pallas_call | solution.py:219
  (54 shorter events, 0.3 us)
Async XLA Ops:
  0.0 9.1 %copy-start.8 = (s32[24,10]{0,1:T(8,128)S(1)}, s32[24,10]{0,1:T(8,128)}, u32[]{:S(2)}) copy-start(s32[24,10]{0,1:T(8,128)} %param.10) | copy-start | bytes 2884
  0.0 9.4 %copy-start.7 = (s32[24,10]{0,1:T(8,128)S(1)}, s32[24,10]{0,1:T(8,128)}, u32[]{:S(2)}) copy-start(s32[24,10]{0,1:T(8,128)} %param.12) | copy-start | bytes 2884
  0.0 9.7 %copy-start.6 = (s32[24,10,3]{0,2,1:T(4,128)S(1)}, s32[24,10,3]{0,2,1:T(4,128)}, u32[]{:S(2)}) copy-start(s32[24,10,3]{0,2,1:T(4,128)} %param.13) | copy-start | bytes 8644
  0.0 10.9 %copy-start.9 = (s32[24,10]{0,1:T(8,128)S(1)}, s32[24,10]{0,1:T(8,128)}, u32[]{:S(2)}) copy-start(s32[24,10]{0,1:T(8,128)} %param.11) | copy-start | bytes 2884
  0.0 11.3 %copy-start.5 = (bf16[24,10,3,200]{3,0,2,1:T(8,128)(2,1)S(1)}, bf16[24,10,3,200]{3,0,2,1:T(8,128)(2,1)}, u32[]{:S(2)}) copy-start(bf16[24,10,3,200]{3,0,2,1:T(8,128)(2,1)} %param.9) | copy-start | bytes 864004
  2.1 19.2 %collective-permute-start.9 = (bf16[4,112,128]{2,1,0:T(8,128)(2,1)S(1)}, bf16[4,112,128]{2,1,0:T(8,128)(2,1)S(1)}, u32[]{:S(2)}, u32[]{:S(2)}) collective-permute-start(bf16[4,112,128]{2,1,0:T(8,128)(2,1)S(1)} %get-tuple-element.17), channel_id=1, source_target_pairs={{0,24},{8,0},{16,8},{24,16},{32,56},{40,32},{48,40},{56,48},{64,88... | collective-permute-start | bytes 344072 | tf_op jit(solution)/shard_map/ppermute | solution.py:25
  6.6 17.7 %collective-permute-start.8 = (bf16[4,112,128]{2,1,0:T(8,128)(2,1)S(1)}, bf16[4,112,128]{2,1,0:T(8,128)(2,1)S(1)}, u32[]{:S(2)}, u32[]{:S(2)}) collective-permute-start(bf16[4,112,128]{2,1,0:T(8,128)(2,1)S(1)} %get-tuple-element.17), channel_id=1, source_target_pairs={{0,8},{8,16},{16,24},{24,0},{32,40},{40,48},{48,56},{56,32},{64,72... | collective-permute-start | bytes 344072 | tf_op jit(solution)/shard_map/ppermute | solution.py:24
  6.7 17.8 %collective-permute-start.1 = (bf16[4,112,128]{2,1,0:T(8,128)(2,1)S(1)}, bf16[4,112,128]{2,1,0:T(8,128)(2,1)S(1)}, u32[]{:S(2)}, u32[]{:S(2)}) collective-permute-start(bf16[4,112,128]{2,1,0:T(8,128)(2,1)S(1)} %get-tuple-element.20), channel_id=1, source_target_pairs={{0,96},{8,104},{16,112},{24,120},{32,0},{40,8},{48,16},{56,24},{64... | collective-permute-start | bytes 344072 | tf_op jit(solution)/shard_map/ppermute | solution.py:25
  9.1 18.3 %collective-permute-start = (bf16[4,112,128]{2,1,0:T(8,128)(2,1)S(1)}, bf16[4,112,128]{2,1,0:T(8,128)(2,1)S(1)}, u32[]{:S(2)}, u32[]{:S(2)}) collective-permute-start(bf16[4,112,128]{2,1,0:T(8,128)(2,1)S(1)} %get-tuple-element.20), channel_id=1, source_target_pairs={{0,32},{8,40},{16,48},{24,56},{32,64},{40,72},{48,80},{56,88},{64,... | collective-permute-start | bytes 344072 | tf_op jit(solution)/shard_map/ppermute | solution.py:24
  15.6 23.1 %all-to-all-start = ((bf16[8,48,768]{2,1,0:T(8,128)(2,1)}), bf16[8,48,768]{2,1,0:T(8,128)(2,1)S(1)}, u32[]{:S(2)}, u32[]{:S(2)}) async-start(bf16[8,48,768]{2,1,0:T(8,128)(2,1)} %bitcast.5), calls=%async_computation | async-start | bytes 1179648 | tf_op jit(solution)/shard_map/all_to_all | solution.py:182
  21.3 15.3 %collective-permute-start.11 = (bf16[2,112,128]{2,1,0:T(8,128)(2,1)S(1)}, bf16[2,112,128]{2,1,0:T(8,128)(2,1)S(1)}, u32[]{:S(2)}, u32[]{:S(2)}) collective-permute-start(bf16[2,112,128]{2,1,0:T(8,128)(2,1)S(1)} %slice.100), channel_id=1, source_target_pairs={{0,24},{8,0},{16,8},{24,16},{32,56},{40,32},{48,40},{56,48},{64,88... | collective-permute-start | bytes 172040 | tf_op jit(solution)/shard_map/ppermute | solution.py:28
  24.3 11.7 %collective-permute-start.10 = (bf16[2,112,128]{2,1,0:T(8,128)(2,1)S(1)}, bf16[2,112,128]{2,1,0:T(8,128)(2,1)S(1)}, u32[]{:S(2)}, u32[]{:S(2)}) collective-permute-start(bf16[2,112,128]{2,1,0:T(8,128)(2,1)S(1)} %slice.99), channel_id=1, source_target_pairs={{0,8},{8,16},{16,24},{24,0},{32,40},{40,48},{48,56},{56,32},{64,72... | collective-permute-start | bytes 172040 | tf_op jit(solution)/shard_map/ppermute | solution.py:27
  24.4 8.1 %collective-permute-start.3 = (bf16[2,112,128]{2,1,0:T(8,128)(2,1)S(1)}, bf16[2,112,128]{2,1,0:T(8,128)(2,1)S(1)}, u32[]{:S(2)}, u32[]{:S(2)}) collective-permute-start(bf16[2,112,128]{2,1,0:T(8,128)(2,1)S(1)} %slice.96), channel_id=1, source_target_pairs={{0,96},{8,104},{16,112},{24,120},{32,0},{40,8},{48,16},{56,24},{64... | collective-permute-start | bytes 172040 | tf_op jit(solution)/shard_map/ppermute | solution.py:28
  27.5 4.5 %collective-permute-start.2 = (bf16[2,112,128]{2,1,0:T(8,128)(2,1)S(1)}, bf16[2,112,128]{2,1,0:T(8,128)(2,1)S(1)}, u32[]{:S(2)}, u32[]{:S(2)}) collective-permute-start(bf16[2,112,128]{2,1,0:T(8,128)(2,1)S(1)} %slice.95), channel_id=1, source_target_pairs={{0,32},{8,40},{16,48},{24,56},{32,64},{40,72},{48,80},{56,88},{64,... | collective-permute-start | bytes 172040 | tf_op jit(solution)/shard_map/ppermute | solution.py:27
  33.2 11.2 %collective-permute-start.5 = (bf16[16,112,128]{2,1,0:T(8,128)(2,1)}, bf16[16,112,128]{2,1,0:T(8,128)(2,1)S(1)}, u32[]{:S(2)}, u32[]{:S(2)}) collective-permute-start(bf16[16,112,128]{2,1,0:T(8,128)(2,1)} %constant_dynamic-update-slice_fusion.refs_0_), channel_id=1, source_target_pairs={{0,24},{8,0},{16,8},{24,16},{32,56},{40,32},{48,40},{56,48},{64,88... | collective-permute-start | bytes 1376264 | tf_op jit(solution)/shard_map/ppermute | solution.py:25
  36.0 11.8 %collective-permute-start.4 = (bf16[16,112,128]{2,1,0:T(8,128)(2,1)}, bf16[16,112,128]{2,1,0:T(8,128)(2,1)S(1)}, u32[]{:S(2)}, u32[]{:S(2)}) collective-permute-start(bf16[16,112,128]{2,1,0:T(8,128)(2,1)} %constant_dynamic-update-slice_fusion.refs_0_), channel_id=1, source_target_pairs={{0,8},{8,16},{16,24},{24,0},{32,40},{40,48},{48,56},{56,32},{64,72... | collective-permute-start | bytes 1376264 | tf_op jit(solution)/shard_map/ppermute | solution.py:24
  37.3 11.3 %collective-permute-start.13 = (bf16[16,112,128]{2,1,0:T(8,128)(2,1)}, bf16[16,112,128]{2,1,0:T(8,128)(2,1)S(1)}, u32[]{:S(2)}, u32[]{:S(2)}) collective-permute-start(bf16[16,112,128]{2,1,0:T(8,128)(2,1)} %constant_dynamic-update-slice_fusion.5.refs_5_), channel_id=1, source_target_pairs={{0,96},{8,104},{16,112},{24,120},{32,0},{40,8},{48,16},{56,24},{64... | collective-permute-start | bytes 1376264 | tf_op jit(solution)/shard_map/ppermute | solution.py:25
  38.0 12.8 %collective-permute-start.12 = (bf16[16,112,128]{2,1,0:T(8,128)(2,1)}, bf16[16,112,128]{2,1,0:T(8,128)(2,1)S(1)}, u32[]{:S(2)}, u32[]{:S(2)}) collective-permute-start(bf16[16,112,128]{2,1,0:T(8,128)(2,1)} %constant_dynamic-update-slice_fusion.5.refs_5_), channel_id=1, source_target_pairs={{0,32},{8,40},{16,48},{24,56},{32,64},{40,72},{48,80},{56,88},{64,... | collective-permute-start | bytes 1376264 | tf_op jit(solution)/shard_map/ppermute | solution.py:24
  38.7 15.4 %copy-start = (bf16[8,48,768]{2,1,0:T(8,128)(2,1)}, bf16[8,48,768]{2,1,0:T(8,128)(2,1)S(1)}, u32[]{:S(2)}) copy-start(bf16[8,48,768]{2,1,0:T(8,128)(2,1)S(1)} %all-to-all-done) | copy-start | bytes 1769476
  44.4 10.0 %copy-start.1 = (bf16[16,112,128]{2,1,0:T(8,128)(2,1)}, bf16[16,112,128]{2,1,0:T(8,128)(2,1)S(1)}, u32[]{:S(2)}) copy-start(bf16[16,112,128]{2,1,0:T(8,128)(2,1)S(1)} %collective-permute-done.5.refs_2_) | copy-start | bytes 1376260
  44.4 12.0 %collective-permute-start.7 = (bf16[8,112,128]{2,1,0:T(8,128)(2,1)S(1)}, bf16[8,112,128]{2,1,0:T(8,128)(2,1)}, u32[]{:S(2)}, u32[]{:S(2)}) collective-permute-start(bf16[8,112,128]{2,1,0:T(8,128)(2,1)S(1)} %slice.98), channel_id=1, source_target_pairs={{0,24},{8,0},{16,8},{24,16},{32,56},{40,32},{48,40},{56,48},{64,88... | collective-permute-start | bytes 688136 | tf_op jit(solution)/shard_map/ppermute | solution.py:28
  47.8 6.6 %copy-start.2 = (bf16[16,112,128]{2,1,0:T(8,128)(2,1)}, bf16[16,112,128]{2,1,0:T(8,128)(2,1)S(1)}, u32[]{:S(2)}) copy-start(bf16[16,112,128]{2,1,0:T(8,128)(2,1)S(1)} %collective-permute-done.4.refs_1_) | copy-start | bytes 1376260
  48.6 7.9 %collective-permute-start.6 = (bf16[8,112,128]{2,1,0:T(8,128)(2,1)}, bf16[8,112,128]{2,1,0:T(8,128)(2,1)}, u32[]{:S(2)}, u32[]{:S(2)}) collective-permute-start(bf16[8,112,128]{2,1,0:T(8,128)(2,1)} %slice.97), channel_id=1, source_target_pairs={{0,8},{8,16},{16,24},{24,0},{32,40},{40,48},{48,56},{56,32},{64,72... | collective-permute-start | bytes 688136 | tf_op jit(solution)/shard_map/ppermute | solution.py:27
  48.6 5.9 %copy-start.3 = (bf16[16,112,128]{2,1,0:T(8,128)(2,1)}, bf16[16,112,128]{2,1,0:T(8,128)(2,1)S(1)}, u32[]{:S(2)}) copy-start(bf16[16,112,128]{2,1,0:T(8,128)(2,1)S(1)} %collective-permute-done.13.refs_7_) | copy-start | bytes 1376260
  49.3 7.1 %collective-permute-start.15 = (bf16[8,112,128]{2,1,0:T(8,128)(2,1)}, bf16[8,112,128]{2,1,0:T(8,128)(2,1)}, u32[]{:S(2)}, u32[]{:S(2)}) collective-permute-start(bf16[8,112,128]{2,1,0:T(8,128)(2,1)} %slice.102), channel_id=1, source_target_pairs={{0,96},{8,104},{16,112},{24,120},{32,0},{40,8},{48,16},{56,24},{64... | collective-permute-start | bytes 688136 | tf_op jit(solution)/shard_map/ppermute | solution.py:28
  50.8 4.9 %copy-start.4 = (bf16[16,112,128]{2,1,0:T(8,128)(2,1)}, bf16[16,112,128]{2,1,0:T(8,128)(2,1)S(1)}, u32[]{:S(2)}) copy-start(bf16[16,112,128]{2,1,0:T(8,128)(2,1)S(1)} %collective-permute-done.12.refs_6_) | copy-start | bytes 1376260
  51.5 6.7 %collective-permute-start.14 = (bf16[8,112,128]{2,1,0:T(8,128)(2,1)}, bf16[8,112,128]{2,1,0:T(8,128)(2,1)}, u32[]{:S(2)}, u32[]{:S(2)}) collective-permute-start(bf16[8,112,128]{2,1,0:T(8,128)(2,1)} %slice.101), channel_id=1, source_target_pairs={{0,32},{8,40},{16,48},{24,56},{32,64},{40,72},{48,80},{56,88},{64,... | collective-permute-start | bytes 688136 | tf_op jit(solution)/shard_map/ppermute | solution.py:27

commit v2 on v1

v2 whole, which is shorter than its diff:
```python
import functools

import jax
import jax.numpy as jnp
from jax import lax
from jax.experimental import pallas as pl
from jax.experimental.pallas import tpu as pltpu
from jax.sharding import PartitionSpec as P

EPS = 1e-06
CAP = 3
SIDE = 4
UNROLL = 16
INFO = 16
PIECES = (2, 2, 4)
FIRST = (0, 32, 64)
STATIONS = (32, 32, 64)


def shifted(axis, step):
    if axis == "x":
        return [(x * SIDE + z, ((x + step) % SIDE) * SIDE + z) for x in range(SIDE) for z in range(SIDE)]
    return [(x * SIDE + z, x * SIDE + (z + step) % SIDE) for x in range(SIDE) for z in range(SIDE)]


def after_kernel(first, second, token, same_first, same_second):
    pass


def ring(first, second, axis, between=None):
    behind_first = lax.ppermute(first, "sta", shifted(axis, 1))
    ahead_second = lax.ppermute(second, "sta", shifted(axis, -1))
    behind_second = lax.ppermute(second, "sta", shifted(axis, 1))
    ahead_first = lax.ppermute(first, "sta", shifted(axis, -1))
    if between is not None:
        behind_first, ahead_second = between(behind_first, ahead_second)
    far_first = lax.ppermute(behind_first, "sta", shifted(axis, 1))
    far_second = lax.ppermute(ahead_second, "sta", shifted(axis, -1))
    return behind_first, behind_second, ahead_first, ahead_second, far_first, far_second


def front_kernel(per_source, here, owner, local, shift, mask, templates, records, outbox, pieces, spread):
    pick_count, channels, own_templates, taps = templates.shape
    rows = pick_count * own_templates
    for c in range(channels):
        for b in range(35):
            block = records[c, :, b * 128 : b * 128 + 128].astype(jnp.float32)
            spread[pl.ds(c * 35 + b, 8, stride=112), :] = block
    for b in range(105, 112):
        spread[pl.ds(b, 8, stride=112), :] = jnp.zeros((8, 128), jnp.float32)
    pieces[...] = spread[...].reshape(pieces.shape).astype(pieces.dtype)

    def flat(table):
        return jnp.concatenate([table[p : p + 1] for p in range(pick_count)], axis=1)

    owner, local, shift = flat(owner[...]), flat(local[...]), flat(shift[...])
    line, column = owner >> 3, owner & 7
    ahead_x = ((line >> 2) - (here[0] >> 2)) & 3
    ahead_z = ((line & 3) - (here[0] & 3)) & 3
    order_x = jnp.where(ahead_x == 3, 1, jnp.where(ahead_x == 0, 0, ahead_x + 1))
    order_z = jnp.where(ahead_z == 3, 1, jnp.where(ahead_z == 0, 0, ahead_z + 1))
    near = 8 * order_x + local
    early = jnp.where(near < 16, 1, 2) == order_z
    stage = jnp.where(order_z == 0, 0, jnp.where(early, 1, 2))
    late = near + jnp.where(order_z == 1, 48, jnp.where(order_z == 2, 80, 96))
    station = jnp.where(stage == 0, near, jnp.where(early, 32 + near, late))
    bins = lax.broadcasted_iota(jnp.int32, (128, rows), 0)
    own = 3 * column + stage == bins
    hot = jnp.where(own, 1.0, 0.0)
    upper = lax.broadcasted_iota(jnp.int32, (rows, rows), 0) < lax.broadcasted_iota(jnp.int32, (rows, rows), 1)
    upper = jnp.where(upper, 1.0, 0.0).astype(jnp.bfloat16)
    before = jnp.dot(hot.astype(jnp.bfloat16), upper, preferred_element_type=jnp.float32)
    held = jnp.broadcast_to(jnp.sum(hot, axis=1, keepdims=True), (128, 128))
    i = lax.broadcasted_iota(jnp.int32, (128, 128), 0)
    j = lax.broadcasted_iota(jnp.int32, (128, 128), 1)
    earlier = jnp.where((((i * 43) >> 7) == ((j * 43) >> 7)) & (j < i), 1.0, 0.0).astype(jnp.bfloat16)
    starts = jnp.dot(earlier, held.astype(jnp.bfloat16), preferred_element_type=jnp.float32)[:, 0:1]
    rank = jnp.sum(jnp.where(own, before + starts, 0.0), axis=0, keepdims=True).astype(jnp.int32)
    position = column * per_source + rank
    template = lax.broadcasted_iota(jnp.int32, (1, rows), 1)
    template = template - own_templates * ((template * 683) >> 14)
    facts = [station, shift, template] + [flat(mask[:, c, :]) for c in range(channels)]
    facts = [fact.astype(jnp.float32) for fact in facts] + [jnp.ones((1, rows), jnp.float32)]
    for k in range(3):
        facts.append(jnp.sum(jnp.where(bins == 3 * column + k, held[:, 0:1], 0.0), axis=0, keepdims=True))
    facts.append(jnp.zeros((16 - len(facts), rows), jnp.float32))
    facts = jnp.concatenate(facts, axis=0).astype(jnp.bfloat16)
    slot = lax.broadcasted_iota(jnp.int32, (outbox.shape[0], rows), 0)
    place = jnp.where(position == slot, 1.0, 0.0).astype(jnp.bfloat16)
    i = lax.broadcasted_iota(jnp.int32, (taps, 256), 0)
    j = lax.broadcasted_iota(jnp.int32, (taps, 256), 1)
    turn = jnp.where(i == 255 - j, 1.0, 0.0).astype(jnp.bfloat16)
    for c in range(channels):
        block = templates[:, c].reshape(rows, taps)
        sent = jnp.dot(block, turn, preferred_element_type=jnp.float32).astype(jnp.bfloat16)
        placed = jnp.dot(place, sent, preferred_element_type=jnp.float32)
        if c == 0:
            i = lax.broadcasted_iota(jnp.int32, (16, 256), 0)
            j = lax.broadcasted_iota(jnp.int32, (16, 256), 1)
            lead = jnp.where(i == j, 1.0, 0.0).astype(jnp.bfloat16)
            known = lax.dot_general(place, facts, (((1,), (1,)), ((), ())), preferred_element_type=jnp.float32)
            placed = placed + jnp.dot(known.astype(jnp.bfloat16), lead, preferred_element_type=jnp.float32)
        outbox[:, 256 * c : 256 * c + 256] = placed.astype(jnp.bfloat16)


def unpack_kernel(inbox, first, second, shapes, marks, power, same_first, same_second):
    slots = inbox.shape[0]
    lanes = lax.broadcasted_iota(jnp.int32, (slots, 128), 1)
    info = inbox[:, 0:128].astype(jnp.float32)
    zero = jnp.zeros((16, 128), jnp.int32)
    for k in range(slots // 128):
        turned = jnp.transpose(info[k * 128 : k * 128 + 128])[:16].astype(jnp.int32)
        marks[:, k * 128 : k * 128 + 128] = turned
    marks[:, slots : slots + 128] = zero
    shapes[pl.ds(8 * slots, 8), :] = jnp.zeros((8, 128), jnp.float32)
    square = jnp.zeros((slots, 128), jnp.float32)
    for k in range(inbox.shape[1] // 128):
        block = inbox[:, k * 128 : k * 128 + 128].astype(jnp.float32)
        if k == 0:
            block = jnp.where(lanes < INFO, 0.0, block)
        shapes[pl.ds(k, slots, stride=8), :] = block
        square = jnp.where(lanes == k // 2, square + jnp.sum(block * block, axis=1, keepdims=True), square)
    for k in range(slots // 128):
        power[:, k * 128 : k * 128 + 128] = jnp.transpose(square[k * 128 : k * 128 + 128])[:8]
    power[:, slots : slots + 128] = jnp.zeros((8, 128), jnp.float32)


def pick_kernel(stage, per_source, taps, marks, power, shapes, *refs):
    pieces = refs[: PIECES[stage]]
    refs = refs[PIECES[stage] :]
    if stage > 0:
        refs = refs[1:]
    total, extra, records, frames, energy, wide, sums, order, sem = refs
    copies = []
    base = 0
    for number, piece in enumerate(pieces):
        size = piece.shape[0]
        copies.append((base, size, pltpu.make_async_copy(piece, records.at[pl.ds(base, size)], sem.at[number])))
        base += size
    for _, _, copy in copies:
        copy.start()
    if stage == 0:
        total[...] = jnp.zeros_like(total)

    taken = jnp.int32(0)
    for source in range(total.shape[0] // 24):
        first = jnp.int32(source * per_source)
        for earlier in range(stage):
            first = first + marks[7 + earlier, source * per_source]
        count = marks[7 + stage, source * per_source]

        def note(k, carry, first=first, taken=taken):
            order[taken + k] = first + k
            return carry

        lax.fori_loop(0, count, note, 0)
        taken = taken + count
    for u in range(UNROLL):
        order[taken + u] = jnp.int32(marks.shape[1] - 128)

    row = lax.broadcasted_iota(jnp.int32, (256, 384), 0)
    column = lax.broadcasted_iota(jnp.int32, (256, 384), 1)
    reach = (column // 128) * 128 + row % 128 - column % 128
    band = jnp.where((reach >= 0) & (reach < taps), 1.0, 0.0).astype(jnp.bfloat16)
    group = sums.shape[0] // 112

    def prepare(step, carry):
        x = records[pl.ds(step * group, group)].reshape(group * 112, 128).astype(jnp.float32)
        wide[...] = x
        square = x * x
        high = square.astype(jnp.bfloat16)
        low = (square - high.astype(jnp.float32)).astype(jnp.bfloat16)
        sums[...] = jnp.dot(jnp.concatenate([high, low], axis=1), band, preferred_element_type=jnp.float32)
        for s in range(group):
            for c in range(3):
                at = s * 112 + c * 35
                slot = (step * group + s) * 3 + c
                energy[slot] = (
                    sums[at : at + 40, 0:128] + sums[at + 1 : at + 41, 128:256] + sums[at + 2 : at + 42, 256:384]
                )
                for q in range(3):
                    frames[slot, 0:40, q * 128 : q * 128 + 128] = wide[at + q : at + q + 40, :].astype(jnp.bfloat16)
        return carry

    for first, size, copy in copies:
        copy.wait()
        lax.fori_loop(first // group, (first + size) // group, prepare, 0)

    across = lax.broadcasted_iota(jnp.int32, (128, 128), 1)
    below = across <= lax.broadcasted_iota(jnp.int32, (128, 128), 0)
    nothing = jnp.zeros((128, 128), jnp.bfloat16)
    lag = lax.broadcasted_iota(jnp.int32, (32, 128), 1)

    def spread(line):
        block = jnp.broadcast_to(line, (128, 128))
        return pltpu.roll(block, 1, 1, stride=1, stride_axis=0).astype(jnp.bfloat16)

    def one_pick(i):
        station = 3 * jnp.maximum(marks[0, i] - FIRST[stage], 0)
        shift = marks[1, i]
        target = marks[2, i] + 24 * jnp.minimum(i // per_source, 7)
        trace = None
        lines = shapes[pl.ds(pl.multiple_of(8 * i, 8), 8), :]
        for c in range(3):
            late = spread(lines[2 * c : 2 * c + 1])
            early = spread(lines[2 * c + 1 : 2 * c + 2])
            toeplitz = jnp.concatenate(
                [jnp.where(below, early, nothing), jnp.where(below, late, early), jnp.where(below, nothing, late)],
                axis=0,
            )
            number = jnp.dot(frames[station + c], toeplitz, preferred_element_type=jnp.float32)[:40]
            level = lax.rsqrt(power[c, i] * energy[station + c] + EPS)
            scaled = number * level * marks[3 + c, i].astype(jnp.float32)
            trace = scaled if trace is None else trace + scaled
        trace = trace.astype(jnp.bfloat16).astype(jnp.float32)
        turned = pltpu.roll(trace, 128 - shift, 1)
        following = pltpu.roll(turned, 39, 0)
        total[target] += jnp.where(lag < 128 - shift, turned[:32], following[:32])

    def several(step, carry):
        for u in range(UNROLL):
            one_pick(order[step * UNROLL + u])
        return carry

    whole = taken // UNROLL
    lax.fori_loop(0, whole, several, 0)

    def rest(step, carry):
        for u in range(4):
            one_pick(order[step * 4 + u])
        return carry

    lax.fori_loop(whole * (UNROLL // 4), (taken + 3) // 4, rest, 0)
    extra[...] = total[: extra.shape[0]].astype(extra.dtype)


def stack_kernel(parts, out, total):
    rows = out.shape[0]
    summed = parts[0].astype(jnp.float32)
    for p in range(1, parts.shape[0]):
        summed = summed + parts[p].astype(jnp.float32)
    cube = summed.reshape(rows, 32, 128)
    square = jnp.sum(jnp.sum(cube * cube, axis=2, keepdims=True), axis=1, keepdims=True)
    level = jnp.sqrt(square / (32 * 128) + EPS)
    total[...] = (cube / level).reshape(rows * 32, 128)
    for b in range(32):
        out[:, b * 128 : b * 128 + 128] = total[pl.ds(b, rows, stride=32), :]


def on_device(records, templates, pick_owner, pick_local, moveout, channel_mask):
    own_templates, pick_count, channels, taps = templates.shape
    columns = lax.axis_size("tpl")
    lines = lax.axis_size("sta")
    rows = own_templates * pick_count
    per_source = CAP * lines
    slots = columns * per_source
    anywhere = pl.BlockSpec(memory_space=pl.ANY)
    vmem, smem = pl.BlockSpec(memory_space=pltpu.VMEM), pl.BlockSpec(memory_space=pltpu.SMEM)

    here = lax.axis_index("sta").astype(jnp.int32).reshape(1)
    outbox, pieces = pl.pallas_call(
        functools.partial(front_kernel, per_source),
        out_shape=(
            jax.ShapeDtypeStruct((slots, channels * 256), jnp.bfloat16),
            jax.ShapeDtypeStruct((records.shape[0], 112, 128), jnp.bfloat16),
        ),
        in_specs=[smem] + [vmem] * 6,
        out_specs=(vmem, vmem),
        scratch_shapes=[pltpu.VMEM((records.shape[0] * 112, 128), jnp.float32)],
        compiler_params=pltpu.CompilerParams(vmem_limit_bytes=60 * 2**20),
    )(
        here,
        pick_owner.T,
        pick_local.T,
        moveout.T,
        channel_mask.transpose(1, 2, 0),
        templates.transpose(1, 2, 0, 3),
        records.transpose(1, 0, 2),
    )
    half = records.shape[0] // 2
    around = ring(pieces[:half], pieces[half:], "x")
    near_first = jnp.concatenate((pieces,) + around[:2])
    near_second = jnp.concatenate(around[2:])
    inbox = lax.all_to_all(
        outbox.reshape(columns, per_source, channels * 256),
        "tpl",
        split_axis=0,
        concat_axis=0,
        tiled=True,
    )
    total_rows = columns * own_templates
    shapes, marks, power, near_first, near_second = pl.pallas_call(
        unpack_kernel,
        out_shape=(
            pltpu.VMEM((slots * 8 + 8, 128), jnp.float32),
            jax.ShapeDtypeStruct((16, slots + 128), jnp.int32),
            jax.ShapeDtypeStruct((8, slots + 128), jnp.float32),
            jax.ShapeDtypeStruct(near_first.shape, near_first.dtype),
            jax.ShapeDtypeStruct(near_second.shape, near_second.dtype),
        ),
        in_specs=[vmem, anywhere, anywhere],
        out_specs=(vmem, vmem, vmem, anywhere, anywhere),
        input_output_aliases={1: 3, 2: 4},
        compiler_params=pltpu.CompilerParams(vmem_limit_bytes=20 * 2**20),
    )(inbox.reshape(slots, channels * 256), near_first, near_second)
    shapes = pltpu.with_memory_space_constraint(shapes, pltpu.VMEM)

    def run_stage(stage, gathered, carried):
        scratch = [
            pltpu.VMEM((STATIONS[stage], 112, 128), jnp.bfloat16),
            pltpu.VMEM((STATIONS[stage] * 3, 48, 384), jnp.bfloat16),
            pltpu.VMEM((STATIONS[stage] * 3, 40, 128), jnp.float32),
            pltpu.VMEM((16 * 112, 128), jnp.float32),
            pltpu.VMEM((16 * 112, 384), jnp.float32),
            pltpu.SMEM((slots + 128,), jnp.int32),
            pltpu.SemaphoreType.DMA((PIECES[stage],)),
        ]
        result = pltpu.VMEM((total_rows, 32, 128), jnp.float32)
        extra = jax.ShapeDtypeStruct((total_rows if stage == 2 else 1, 32, 128), jnp.bfloat16)
        carried = [pltpu.with_memory_space_constraint(p, pltpu.VMEM) for p in carried]
        return pl.pallas_call(
            functools.partial(pick_kernel, stage, per_source, taps),
            out_shape=(result, extra),
            in_specs=[smem, smem, vmem] + [anywhere] * PIECES[stage] + [vmem] * len(carried),
            out_specs=(vmem, vmem),
            scratch_shapes=scratch,
            input_output_aliases={3 + PIECES[stage]: 0} if carried else {},
            cost_estimate=pl.CostEstimate(flops=0, bytes_accessed=(30, 50, 30)[stage] * 10**6, transcendentals=0),
            compiler_params=pltpu.CompilerParams(vmem_limit_bytes=48 * 2**20),
        )(marks, power, shapes, *gathered, *carried)

    partial, token = run_stage(0, (near_first, near_second), ())

    def after(first, second):
        return pl.pallas_call(
            after_kernel,
            out_shape=tuple(jax.ShapeDtypeStruct(x.shape, x.dtype) for x in (first, second)),
            in_specs=[anywhere] * 3,
            out_specs=(anywhere, anywhere),
            input_output_aliases={0: 0, 1: 1},
            compiler_params=pltpu.CompilerParams(vmem_limit_bytes=2**20),
        )(first, second, token)

    far = ring(near_first, near_second, "z", after)
    partial, _ = run_stage(1, (far[0], far[3]), (partial,))
    _, partial = run_stage(2, (far[1], far[2], far[4], far[5]), (partial,))

    returned = lax.all_to_all(
        partial.reshape(columns, own_templates * 32, 128), "tpl", split_axis=0, concat_axis=0, tiled=True
    )
    return pl.pallas_call(
        stack_kernel,
        out_shape=jax.ShapeDtypeStruct((own_templates, 4096), jnp.float32),
        in_specs=[vmem],
        out_specs=vmem,
        scratch_shapes=[pltpu.VMEM((own_templates * 32, 128), jnp.float32)],
        compiler_params=pltpu.CompilerParams(vmem_limit_bytes=20 * 2**20),
    )(returned)


def solution(mesh):
    return jax.shard_map(
        on_device,
        mesh=mesh,
        in_specs=(
            P(("sta", "tpl"), None, None),
            P(("sta", "tpl"), None, None, None),
            P(("sta", "tpl"), None),
            P(("sta", "tpl"), None),
            P(("sta", "tpl"), None),
            P(("sta", "tpl"), None, None),
        ),
        out_specs=P(("sta", "tpl"), None),
        check_vma=False,
    )
```

time: 126 us -> 104 us (0.83)
  local copies, waits for them, and re-layouts: 16.2 us -> 1.77 us
  starting transfers between devices: 28.1 us -> 23.3 us
  Pallas kernels: 36.1 us -> 39.9 us
  blocking collectives: 32.8 us -> 29.8 us
  other arithmetic: 3.14 us -> 1.05 us
    unnamed x33 -> x2, local copies, waits for them, and re-layouts: 7.73 us -> 0.8 us
    ppermute x16 -> x12, starting transfers between devices: 22.4 us -> 17.3 us  [the longest x2 5.38 us: ring(): ahead_first = lax.ppermute(first, 'sta', shifted(axis, -1))]
    pallas_call x1 -> x6, Pallas kernels: 34.8 us -> 38.6 us  [the longest x3 34.8 us: run_stage(): pl.pallas_call(functools.partial(pick_kernel, stage, per_source, taps), o...]
    all_to_all x1, blocking collectives: 32.8 us -> 29.8 us  [on_device(): lax.all_to_all(partial.reshape(columns, own_templates * 32, 128), 'tpl',...]
    reshape x9 -> x0, local copies, waits for them, and re-layouts: 2.37 us -> none  [the longest x1 0.73 us: on_device(): jnp.pad(jnp.sum(wide * wide, axis=2), ((0, 0), (0, 1))).reshape(slots * 4)]
    slice x9 -> x1, local copies, waits for them, and re-layouts: 3.02 us -> 0.97 us  [on_device(): around = ring(pieces[:half], pieces[half:], 'x')]
    concatenate x4 -> x0, local copies, waits for them, and re-layouts: 1.44 us -> none  [the longest x1 0.63 us: on_device(): by_x = jnp.concatenate((pieces[:half],) + ring(pieces[:half], 'x'))]
    ppermute x16 -> x12, waiting for transfers between devices: 9.28 us -> 8.23 us  [the longest x2 7.57 us: ring(): far_first = lax.ppermute(behind_first, 'sta', shifted(axis, 1))]
  transfers between devices with their start and end apart: 17 -> 13, of which waited for: 3 -> 3; matrix products, arithmetic and copies ran while one was open for 15% -> 2% of each run, Pallas kernels for 0% -> 18%
where the time goes in v2:
time: 104 us
  Pallas kernels  39.9 us (38%)
  blocking collectives  29.8 us (29%)
  starting transfers between devices  23.3 us (22%)
  waiting for transfers between devices  8.23 us (8%)
  local copies, waits for them, and re-layouts  1.77 us (2%)
  other arithmetic  1.05 us (1%)
    pallas_call x3, Pallas kernels, run_stage(): pl.pallas_call(functools.partial(pick_kernel, stage, per_source, taps), o...  34.8 us
    all_to_all x1, blocking collectives, on_device(): lax.all_to_all(partial.reshape(columns, own_templates * 32, 128), 'tpl',...  29.8 us
    ppermute x2, waiting for transfers between devices, ring(): far_first = lax.ppermute(behind_first, 'sta', shifted(axis, 1))  7.57 us
    all_to_all x1, starting transfers between devices, on_device(): lax.all_to_all(outbox.reshape(columns, per_source, channels * 256), 'tpl'...  5.97 us
    ppermute x2, starting transfers between devices, ring(): ahead_first = lax.ppermute(first, 'sta', shifted(axis, -1))  5.38 us
    ppermute x2, starting transfers between devices, ring(): far_second = lax.ppermute(ahead_second, 'sta', shifted(axis, -1))  5.34 us
    ppermute x2, starting transfers between devices, ring(): ahead_second = lax.ppermute(second, 'sta', shifted(axis, -1))  5.27 us
    pallas_call x1, Pallas kernels, on_device(): pl.pallas_call(functools.partial(front_kernel, per_source), out_shape=(ja...  3.25 us
  transfers between devices with their start and end apart: 13, of which 3 were waited for; matrix products, arithmetic and copies ran while one was open for 2% of the time, Pallas kernels for 18%

profile of v2, /device:TPU:1, one launch (start us, length us, event | category | flops | bytes accessed | tf_op | source)
XLA Modules:
  0.0 104.2 jit_solution(2117993104488077282)
XLA Ops:
  0.0 3.2 %shard_map.64 = (bf16[384,768]{1,0:T(8,128)(2,1)}, bf16[8,112,128]{2,1,0:T(8,128)(2,1)}) custom-call(s32[1]{0:T(128)} %bitcast.here, s32[10,24]{1,0:T(8,128)} %bitcast.16, s32[10,24]{1,0:T(8,128)} %bitcast.17, s32[10,24]{1,0:T(8,128)} %bitcast.18, s32[10,3,24]{2,1,0:T(4,128)} %bitcast.15, bf16[10,3,24,200]{3,2,1,0:T(8,128)(2,1)} %bitcast.13, ...), custom_call_target="tpu_custom_call" | custom-call | tf_op jit(solution)/shard_map/pallas_call | solution.py:261
  3.2 6.0 %all-to-all-start = ((bf16[8,48,768]{2,1,0:T(8,128)(2,1)}), bf16[8,48,768]{2,1,0:T(8,128)(2,1)S(1)}, u32[]{:S(2)}, u32[]{:S(2)}) async-start(bf16[8,48,768]{2,1,0:T(8,128)(2,1)} %bitcast.12), calls=%async_computation | async-start | bytes 1179648 | tf_op jit(solution)/shard_map/all_to_all | solution.py:284
  9.2 1.0 fusion
  10.2 1.3 %collective-permute-start = (bf16[4,112,128]{2,1,0:T(8,128)(2,1)S(1)}, bf16[4,112,128]{2,1,0:T(8,128)(2,1)S(1)}, u32[]{:S(2)}, u32[]{:S(2)}) collective-permute-start(bf16[4,112,128]{2,1,0:T(8,128)(2,1)S(1)} %get-tuple-element.31), channel_id=1, source_target_pairs={{0,32},{8,40},{16,48},{24,56},{32,64},{40,72},{48,80},{56,88},{64,... | collective-permute-start | bytes 344072 | tf_op jit(solution)/shard_map/ppermute | solution.py:31
  11.5 1.5 %collective-permute-start.3 = (bf16[4,112,128]{2,1,0:T(8,128)(2,1)S(1)}, bf16[4,112,128]{2,1,0:T(8,128)(2,1)S(1)}, u32[]{:S(2)}, u32[]{:S(2)}) collective-permute-start(bf16[4,112,128]{2,1,0:T(8,128)(2,1)S(1)} %get-tuple-element.32), channel_id=1, source_target_pairs={{0,96},{8,104},{16,112},{24,120},{32,0},{40,8},{48,16},{56,24},{64... | collective-permute-start | bytes 344072 | tf_op jit(solution)/shard_map/ppermute | solution.py:32
  12.9 0.0 collective-permute-start.1
  12.9 2.7 %collective-permute-start.2 = (bf16[4,112,128]{2,1,0:T(8,128)(2,1)S(1)}, bf16[4,112,128]{2,1,0:T(8,128)(2,1)S(1)}, u32[]{:S(2)}, u32[]{:S(2)}) collective-permute-start(bf16[4,112,128]{2,1,0:T(8,128)(2,1)S(1)} %get-tuple-element.31), channel_id=1, source_target_pairs={{0,96},{8,104},{16,112},{24,120},{32,0},{40,8},{48,16},{56,24},{64... | collective-permute-start | bytes 344072 | tf_op jit(solution)/shard_map/ppermute | solution.py:34
  15.6 0.6 collective-permute-done
  16.2 0.0 collective-permute-start.4
  16.3 0.0 collective-permute-done.3
  16.3 2.7 %collective-permute-start.5 = (bf16[4,112,128]{2,1,0:T(8,128)(2,1)S(1)}, bf16[4,112,128]{2,1,0:T(8,128)(2,1)S(1)}, u32[]{:S(2)}, u32[]{:S(2)}) collective-permute-start(bf16[4,112,128]{2,1,0:T(8,128)(2,1)S(1)} %collective-permute-done.3), channel_id=1, source_target_pairs={{0,96},{8,104},{16,112},{24,120},{32,0},{40,8},{48,16},{56,24},{64... | collective-permute-start | bytes 344072 | tf_op jit(solution)/shard_map/ppermute | solution.py:38
  18.9 0.0 collective-permute-done.1
  18.9 1.0 pad_maximum_fusion.first
  19.9 0.0 collective-permute-done.2
  19.9 1.2 %collective-permute-done.4 = bf16[4,112,128]{2,1,0:T(8,128)(2,1)S(1)} collective-permute-done((bf16[4,112,128]{2,1,0:T(8,128)(2,1)S(1)}, bf16[4,112,128]{2,1,0:T(8,128)(2,1)S(1)}, u32[]{:S(2)}, u32[]{:S(2)}) %collective-permute-start.4) | collective-permute-done | bytes 114720 | tf_op jit(solution)/shard_map/ppermute | solution.py:37
  21.1 0.0 collective-permute-done.5
  21.1 0.1 pad_maximum_fusion.1.second
  21.2 0.0 all-to-all-done
  21.2 0.6 shard_map.65
  21.8 3.8 %collective-permute-start.9 = (bf16[16,112,128]{2,1,0:T(8,128)(2,1)S(1)}, bf16[16,112,128]{2,1,0:T(8,128)(2,1)S(1)}, u32[]{:S(2)}, u32[]{:S(2)}) collective-permute-start(bf16[16,112,128]{2,1,0:T(8,128)(2,1)S(1)} %get-tuple-element.23.refs_1_), channel_id=1, source_target_pairs={{0,24},{8,0},{16,8},{24,16},{32,56},{40,32},{48,40},{56,48},{64,88... | collective-permute-start | bytes 1376264 | tf_op jit(solution)/shard_map/ppermute | solution.py:32
  25.6 0.0 collective-permute-start.8
  25.6 0.0 collective-permute-start.6
  25.6 2.7 %collective-permute-start.7 = (bf16[16,112,128]{2,1,0:T(8,128)(2,1)S(1)}, bf16[16,112,128]{2,1,0:T(8,128)(2,1)S(1)}, u32[]{:S(2)}, u32[]{:S(2)}) collective-permute-start(bf16[16,112,128]{2,1,0:T(8,128)(2,1)S(1)} %get-tuple-element.24.refs_0_), channel_id=1, source_target_pairs={{0,24},{8,0},{16,8},{24,16},{32,56},{40,32},{48,40},{56,48},{64,88... | collective-permute-start | bytes 1376264 | tf_op jit(solution)/shard_map/ppermute | solution.py:34
  28.3 8.8 %shard_map.66 = (f32[192,32,128]{2,1,0:T(8,128)S(1)}, bf16[1,32,128]{2,1,0:T(8,128)(2,1)S(1)}) custom-call(s32[16,512]{1,0:T(8,128)S(1)} %get-tuple-element.20.marks, f32[8,512]{1,0:T(8,128)S(1)} %get-tuple-element.21.power, f32[3080,128]{1,0:T(8,128)S(1)} %get-tuple-element.22.shapes, bf16[16,112,128]{2,1,0:T(8,128)(2,1)S(1)} %get-tuple-element.24.refs_0_, ...), custom_call_target="tpu_custom_call" | custom-call | bytes 30000000 | tf_op jit(solution)/shard_map/pallas_call | solution.py:321
  37.1 0.0 collective-permute-done.9.second
  37.1 0.0 collective-permute-done.8.first
  37.2 0.1 collective-permute-start.10
  37.2 2.7 %collective-permute-start.11 = (bf16[16,112,128]{2,1,0:T(8,128)(2,1)S(1)}, bf16[16,112,128]{2,1,0:T(8,128)(2,1)S(1)}, u32[]{:S(2)}, u32[]{:S(2)}) collective-permute-start(bf16[16,112,128]{2,1,0:T(8,128)(2,1)S(1)} %get-tuple-element.27.refs_1_), channel_id=1, source_target_pairs={{0,24},{8,0},{16,8},{24,16},{32,56},{40,32},{48,40},{56,48},{64,88... | collective-permute-start | bytes 1376264 | tf_op jit(solution)/shard_map/ppermute | solution.py:38
  39.9 9.9 %shard_map.68 = (f32[192,32,128]{2,1,0:T(8,128)S(1)}, bf16[1,32,128]{2,1,0:T(8,128)(2,1)}) custom-call(s32[16,512]{1,0:T(8,128)S(1)} %get-tuple-element.20.marks, f32[8,512]{1,0:T(8,128)S(1)} %get-tuple-element.21.power, f32[3080,128]{1,0:T(8,128)S(1)} %get-tuple-element.22.shapes, ...), custom_call_target="tpu_custom_call", output_to_operand_aliasing={{0}: (5, {})} | custom-call | bytes 50000000 | tf_op jit(solution)/shard_map/pallas_call | solution.py:321
  49.8 0.0 collective-permute-done.6.refs_0_
  49.8 0.0 collective-permute-done.7.refs_1_
  49.8 6.4 %collective-permute-done.10.refs_2_ = bf16[16,112,128]{2,1,0:T(8,128)(2,1)S(1)} collective-permute-done((bf16[16,112,128]{2,1,0:T(8,128)(2,1)S(1)}, bf16[16,112,128]{2,1,0:T(8,128)(2,1)S(1)}, u32[]{:S(2)}, u32[]{:S(2)}) %collective-permute-start.10) | collective-permute-done | bytes 458784 | tf_op jit(solution)/shard_map/ppermute | solution.py:37
  56.2 0.0 collective-permute-done.11.refs_3_
  56.2 0.0 copy-start
  56.2 0.8 copy-done
  57.0 16.1 %shard_map.69 = (f32[192,32,128]{2,1,0:T(8,128)S(1)}, bf16[192,32,128]{2,1,0:T(8,128)(2,1)}) custom-call(s32[16,512]{1,0:T(8,128)S(1)} %get-tuple-element.20.marks, f32[8,512]{1,0:T(8,128)S(1)} %get-tuple-element.21.power, f32[3080,128]{1,0:T(8,128)S(1)} %get-tuple-element.22.shapes, ...), custom_call_target="tpu_custom_call", output_to_operand_aliasing={{0}: (7, {})} | custom-call | bytes 30000000 | tf_op jit(solution)/shard_map/pallas_call | solution.py:321
  73.1 29.8 %all_to_all.10.parts = bf16[8,768,128]{2,1,0:T(8,128)(2,1)S(1)} all-to-all(bf16[8,768,128]{2,1,0:T(8,128)(2,1)} %bitcast.11), channel_id=1, replica_groups=mesh['sta'=16,'tpl'=8] {'tpl'}, dimensions={0} | all-to-all | bytes 3145728 | tf_op jit(solution)/shard_map/all_to_all | solution.py:348
  102.9 1.3 %shard_map.70 = f32[24,4096]{1,0:T(8,128)} custom-call(bf16[8,768,128]{2,1,0:T(8,128)(2,1)S(1)} %all_to_all.10.parts), custom_call_target="tpu_custom_call" | custom-call | tf_op jit(solution)/shard_map/pallas_call | solution.py:351
  (1 shorter events, 0.0 us)
Async XLA Ops:
  3.2 17.9 %all-to-all-start = ((bf16[8,48,768]{2,1,0:T(8,128)(2,1)}), bf16[8,48,768]{2,1,0:T(8,128)(2,1)S(1)}, u32[]{:S(2)}, u32[]{:S(2)}) async-start(bf16[8,48,768]{2,1,0:T(8,128)(2,1)} %bitcast.12), calls=%async_computation | async-start | bytes 1179648 | tf_op jit(solution)/shard_map/all_to_all | solution.py:284
  10.2 6.1 %collective-permute-start = (bf16[4,112,128]{2,1,0:T(8,128)(2,1)S(1)}, bf16[4,112,128]{2,1,0:T(8,128)(2,1)S(1)}, u32[]{:S(2)}, u32[]{:S(2)}) collective-permute-start(bf16[4,112,128]{2,1,0:T(8,128)(2,1)S(1)} %get-tuple-element.31), channel_id=1, source_target_pairs={{0,32},{8,40},{16,48},{24,56},{32,64},{40,72},{48,80},{56,88},{64,... | collective-permute-start | bytes 344072 | tf_op jit(solution)/shard_map/ppermute | solution.py:31
  11.5 4.8 %collective-permute-start.3 = (bf16[4,112,128]{2,1,0:T(8,128)(2,1)S(1)}, bf16[4,112,128]{2,1,0:T(8,128)(2,1)S(1)}, u32[]{:S(2)}, u32[]{:S(2)}) collective-permute-start(bf16[4,112,128]{2,1,0:T(8,128)(2,1)S(1)} %get-tuple-element.32), channel_id=1, source_target_pairs={{0,96},{8,104},{16,112},{24,120},{32,0},{40,8},{48,16},{56,24},{64... | collective-permute-start | bytes 344072 | tf_op jit(solution)/shard_map/ppermute | solution.py:32
  12.9 6.0 %collective-permute-start.1 = (bf16[4,112,128]{2,1,0:T(8,128)(2,1)S(1)}, bf16[4,112,128]{2,1,0:T(8,128)(2,1)S(1)}, u32[]{:S(2)}, u32[]{:S(2)}) collective-permute-start(bf16[4,112,128]{2,1,0:T(8,128)(2,1)S(1)} %get-tuple-element.32), channel_id=1, source_target_pairs={{0,32},{8,40},{16,48},{24,56},{32,64},{40,72},{48,80},{56,88},{64,... | collective-permute-start | bytes 344072 | tf_op jit(solution)/shard_map/ppermute | solution.py:33
  12.9 7.0 %collective-permute-start.2 = (bf16[4,112,128]{2,1,0:T(8,128)(2,1)S(1)}, bf16[4,112,128]{2,1,0:T(8,128)(2,1)S(1)}, u32[]{:S(2)}, u32[]{:S(2)}) collective-permute-start(bf16[4,112,128]{2,1,0:T(8,128)(2,1)S(1)} %get-tuple-element.31), channel_id=1, source_target_pairs={{0,96},{8,104},{16,112},{24,120},{32,0},{40,8},{48,16},{56,24},{64... | collective-permute-start | bytes 344072 | tf_op jit(solution)/shard_map/ppermute | solution.py:34
  16.2 4.9 %collective-permute-start.4 = (bf16[4,112,128]{2,1,0:T(8,128)(2,1)S(1)}, bf16[4,112,128]{2,1,0:T(8,128)(2,1)S(1)}, u32[]{:S(2)}, u32[]{:S(2)}) collective-permute-start(bf16[4,112,128]{2,1,0:T(8,128)(2,1)S(1)} %collective-permute-done), channel_id=1, source_target_pairs={{0,32},{8,40},{16,48},{24,56},{32,64},{40,72},{48,80},{56,88},{64,... | collective-permute-start | bytes 344072 | tf_op jit(solution)/shard_map/ppermute | solution.py:37
  16.3 4.8 %collective-permute-start.5 = (bf16[4,112,128]{2,1,0:T(8,128)(2,1)S(1)}, bf16[4,112,128]{2,1,0:T(8,128)(2,1)S(1)}, u32[]{:S(2)}, u32[]{:S(2)}) collective-permute-start(bf16[4,112,128]{2,1,0:T(8,128)(2,1)S(1)} %collective-permute-done.3), channel_id=1, source_target_pairs={{0,96},{8,104},{16,112},{24,120},{32,0},{40,8},{48,16},{56,24},{64... | collective-permute-start | bytes 344072 | tf_op jit(solution)/shard_map/ppermute | solution.py:38
  21.8 15.4 %collective-permute-start.9 = (bf16[16,112,128]{2,1,0:T(8,128)(2,1)S(1)}, bf16[16,112,128]{2,1,0:T(8,128)(2,1)S(1)}, u32[]{:S(2)}, u32[]{:S(2)}) collective-permute-start(bf16[16,112,128]{2,1,0:T(8,128)(2,1)S(1)} %get-tuple-element.23.refs_1_), channel_id=1, source_target_pairs={{0,24},{8,0},{16,8},{24,16},{32,56},{40,32},{48,40},{56,48},{64,88... | collective-permute-start | bytes 1376264 | tf_op jit(solution)/shard_map/ppermute | solution.py:32
  25.6 11.6 %collective-permute-start.8 = (bf16[16,112,128]{2,1,0:T(8,128)(2,1)S(1)}, bf16[16,112,128]{2,1,0:T(8,128)(2,1)S(1)}, u32[]{:S(2)}, u32[]{:S(2)}) collective-permute-start(bf16[16,112,128]{2,1,0:T(8,128)(2,1)S(1)} %get-tuple-element.24.refs_0_), channel_id=1, source_target_pairs={{0,8},{8,16},{16,24},{24,0},{32,40},{40,48},{48,56},{56,32},{64,72... | collective-permute-start | bytes 1376264 | tf_op jit(solution)/shard_map/ppermute | solution.py:31
  25.6 24.2 %collective-permute-start.6 = (bf16[16,112,128]{2,1,0:T(8,128)(2,1)S(1)}, bf16[16,112,128]{2,1,0:T(8,128)(2,1)S(1)}, u32[]{:S(2)}, u32[]{:S(2)}) collective-permute-start(bf16[16,112,128]{2,1,0:T(8,128)(2,1)S(1)} %get-tuple-element.23.refs_1_), channel_id=1, source_target_pairs={{0,8},{8,16},{16,24},{24,0},{32,40},{40,48},{48,56},{56,32},{64,72... | collective-permute-start | bytes 1376264 | tf_op jit(solution)/shard_map/ppermute | solution.py:33
  25.6 24.2 %collective-permute-start.7 = (bf16[16,112,128]{2,1,0:T(8,128)(2,1)S(1)}, bf16[16,112,128]{2,1,0:T(8,128)(2,1)S(1)}, u32[]{:S(2)}, u32[]{:S(2)}) collective-permute-start(bf16[16,112,128]{2,1,0:T(8,128)(2,1)S(1)} %get-tuple-element.24.refs_0_), channel_id=1, source_target_pairs={{0,24},{8,0},{16,8},{24,16},{32,56},{40,32},{48,40},{56,48},{64,88... | collective-permute-start | bytes 1376264 | tf_op jit(solution)/shard_map/ppermute | solution.py:34
  37.2 19.1 %collective-permute-start.10 = (bf16[16,112,128]{2,1,0:T(8,128)(2,1)S(1)}, bf16[16,112,128]{2,1,0:T(8,128)(2,1)S(1)}, u32[]{:S(2)}, u32[]{:S(2)}) collective-permute-start(bf16[16,112,128]{2,1,0:T(8,128)(2,1)S(1)} %get-tuple-element.26.refs_0_), channel_id=1, source_target_pairs={{0,8},{8,16},{16,24},{24,0},{32,40},{40,48},{48,56},{56,32},{64,72... | collective-permute-start | bytes 1376264 | tf_op jit(solution)/shard_map/ppermute | solution.py:37
  37.2 19.0 %collective-permute-start.11 = (bf16[16,112,128]{2,1,0:T(8,128)(2,1)S(1)}, bf16[16,112,128]{2,1,0:T(8,128)(2,1)S(1)}, u32[]{:S(2)}, u32[]{:S(2)}) collective-permute-start(bf16[16,112,128]{2,1,0:T(8,128)(2,1)S(1)} %get-tuple-element.27.refs_1_), channel_id=1, source_target_pairs={{0,24},{8,0},{16,8},{24,16},{32,56},{40,32},{48,40},{56,48},{64,88... | collective-permute-start | bytes 1376264 | tf_op jit(solution)/shard_map/ppermute | solution.py:38
  56.2 0.8 copy-start

commit v3 on v2

--- a/solution.py
+++ b/solution.py
@@ -12,9 +12,9 @@
 SIDE = 4
 UNROLL = 16
 INFO = 16
-PIECES = (2, 2, 4)
-FIRST = (0, 32, 64)
-STATIONS = (32, 32, 64)
+PIECES = (2, 2, 2, 2)
+FIRST = (0, 32, 64, 96)
+STATIONS = (32, 32, 32, 32)
 
 
 def shifted(axis, step):
@@ -39,7 +39,7 @@
     return behind_first, behind_second, ahead_first, ahead_second, far_first, far_second
 
 
-def front_kernel(per_source, here, owner, local, shift, mask, templates, records, outbox, pieces, spread):
+def front_kernel(per_source, here, owner, local, shift, mask, templates, records, outbox, first, second, spread):
     pick_count, channels, own_templates, taps = templates.shape
     rows = pick_count * own_templates
     for c in range(channels):
@@ -48,7 +48,9 @@
             spread[pl.ds(c * 35 + b, 8, stride=112), :] = block
     for b in range(105, 112):
         spread[pl.ds(b, 8, stride=112), :] = jnp.zeros((8, 128), jnp.float32)
-    pieces[...] = spread[...].reshape(pieces.shape).astype(pieces.dtype)
+    half = first.shape[0] * 112
+    first[...] = spread[:half].reshape(first.shape).astype(first.dtype)
+    second[...] = spread[half:].reshape(second.shape).astype(second.dtype)
 
     def flat(table):
         return jnp.concatenate([table[p : p + 1] for p in range(pick_count)], axis=1)
@@ -61,11 +63,11 @@
     order_z = jnp.where(ahead_z == 3, 1, jnp.where(ahead_z == 0, 0, ahead_z + 1))
     near = 8 * order_x + local
     early = jnp.where(near < 16, 1, 2) == order_z
-    stage = jnp.where(order_z == 0, 0, jnp.where(early, 1, 2))
+    stage = jnp.where(order_z == 0, 0, jnp.where(early, 1, jnp.where(order_z == 3, 3, 2)))
     late = near + jnp.where(order_z == 1, 48, jnp.where(order_z == 2, 80, 96))
     station = jnp.where(stage == 0, near, jnp.where(early, 32 + near, late))
     bins = lax.broadcasted_iota(jnp.int32, (128, rows), 0)
-    own = 3 * column + stage == bins
+    own = 4 * column + stage == bins
     hot = jnp.where(own, 1.0, 0.0)
     upper = lax.broadcasted_iota(jnp.int32, (rows, rows), 0) < lax.broadcasted_iota(jnp.int32, (rows, rows), 1)
     upper = jnp.where(upper, 1.0, 0.0).astype(jnp.bfloat16)
@@ -73,7 +75,7 @@
     held = jnp.broadcast_to(jnp.sum(hot, axis=1, keepdims=True), (128, 128))
     i = lax.broadcasted_iota(jnp.int32, (128, 128), 0)
     j = lax.broadcasted_iota(jnp.int32, (128, 128), 1)
-    earlier = jnp.where((((i * 43) >> 7) == ((j * 43) >> 7)) & (j < i), 1.0, 0.0).astype(jnp.bfloat16)
+    earlier = jnp.where(((i >> 2) == (j >> 2)) & (j < i), 1.0, 0.0).astype(jnp.bfloat16)
     starts = jnp.dot(earlier, held.astype(jnp.bfloat16), preferred_element_type=jnp.float32)[:, 0:1]
     rank = jnp.sum(jnp.where(own, before + starts, 0.0), axis=0, keepdims=True).astype(jnp.int32)
     position = column * per_source + rank
@@ -81,8 +83,8 @@
     template = template - own_templates * ((template * 683) >> 14)
     facts = [station, shift, template] + [flat(mask[:, c, :]) for c in range(channels)]
     facts = [fact.astype(jnp.float32) for fact in facts] + [jnp.ones((1, rows), jnp.float32)]
-    for k in range(3):
-        facts.append(jnp.sum(jnp.where(bins == 3 * column + k, held[:, 0:1], 0.0), axis=0, keepdims=True))
+    for k in range(4):
+        facts.append(jnp.sum(jnp.where(bins == 4 * column + k, held[:, 0:1], 0.0), axis=0, keepdims=True))
     facts.append(jnp.zeros((16 - len(facts), rows), jnp.float32))
     facts = jnp.concatenate(facts, axis=0).astype(jnp.bfloat16)
     slot = lax.broadcasted_iota(jnp.int32, (outbox.shape[0], rows), 0)
@@ -158,10 +160,14 @@
     for u in range(UNROLL):
         order[taken + u] = jnp.int32(marks.shape[1] - 128)
 
-    row = lax.broadcasted_iota(jnp.int32, (256, 384), 0)
-    column = lax.broadcasted_iota(jnp.int32, (256, 384), 1)
-    reach = (column // 128) * 128 + row % 128 - column % 128
-    band = jnp.where((reach >= 0) & (reach < taps), 1.0, 0.0).astype(jnp.bfloat16)
+    row = lax.broadcasted_iota(jnp.int32, (256, 256), 0) % 128
+    column = lax.broadcasted_iota(jnp.int32, (256, 256), 1) % 128
+    tail = taps - 128
+    suffix = row >= column
+    prefix = ((column < 128 - tail) & (row - column < tail)) | (column - row > 128 - tail)
+    left = lax.broadcasted_iota(jnp.int32, (256, 256), 1) < 128
+    band = jnp.where((left & suffix) | (~left & prefix), 1.0, 0.0).astype(jnp.bfloat16)
+    near_side = lax.broadcasted_iota(jnp.int32, (40, 128), 1) < 128 - tail
     group = sums.shape[0] // 112
 
     def prepare(step, carry):
@@ -175,9 +181,11 @@
             for c in range(3):
                 at = s * 112 + c * 35
                 slot = (step * group + s) * 3 + c
-                energy[slot] = (
-                    sums[at : at + 40, 0:128] + sums[at + 1 : at + 41, 128:256] + sums[at + 2 : at + 42, 256:384]
+                whole = jnp.broadcast_to(sums[at + 1 : at + 41, 0:128][:, 0:1], (40, 128))
+                ending = jnp.where(
+                    near_side, sums[at + 1 : at + 41, 128:256], whole + sums[at + 2 : at + 42, 128:256]
                 )
+                energy[slot] = sums[at : at + 40, 0:128] + ending
                 for q in range(3):
                     frames[slot, 0:40, q * 128 : q * 128 + 128] = wide[at + q : at + q + 40, :].astype(jnp.bfloat16)
         return carry
@@ -258,14 +266,16 @@
     vmem, smem = pl.BlockSpec(memory_space=pltpu.VMEM), pl.BlockSpec(memory_space=pltpu.SMEM)
 
     here = lax.axis_index("sta").astype(jnp.int32).reshape(1)
-    outbox, pieces = pl.pallas_call(
+    half = records.shape[0] // 2
+    outbox, first, second = pl.pallas_call(
         functools.partial(front_kernel, per_source),
         out_shape=(
             jax.ShapeDtypeStruct((slots, channels * 256), jnp.bfloat16),
-            jax.ShapeDtypeStruct((records.shape[0], 112, 128), jnp.bfloat16),
+            jax.ShapeDtypeStruct((half, 112, 128), jnp.bfloat16),
+            jax.ShapeDtypeStruct((half, 112, 128), jnp.bfloat16),
         ),
         in_specs=[smem] + [vmem] * 6,
-        out_specs=(vmem, vmem),
+        out_specs=(vmem, vmem, vmem),
         scratch_shapes=[pltpu.VMEM((records.shape[0] * 112, 128), jnp.float32)],
         compiler_params=pltpu.CompilerParams(vmem_limit_bytes=60 * 2**20),
     )(
@@ -277,9 +287,8 @@
         templates.transpose(1, 2, 0, 3),
         records.transpose(1, 0, 2),
     )
-    half = records.shape[0] // 2
-    around = ring(pieces[:half], pieces[half:], "x")
-    near_first = jnp.concatenate((pieces,) + around[:2])
+    around = ring(first, second, "x")
+    near_first = jnp.concatenate((first, second) + around[:2])
     near_second = jnp.concatenate(around[2:])
     inbox = lax.all_to_all(
         outbox.reshape(columns, per_source, channels * 256),
@@ -295,8 +304,8 @@
             pltpu.VMEM((slots * 8 + 8, 128), jnp.float32),
             jax.ShapeDtypeStruct((16, slots + 128), jnp.int32),
             jax.ShapeDtypeStruct((8, slots + 128), jnp.float32),
-            jax.ShapeDtypeStruct(near_first.shape, near_first.dtype),
-            jax.ShapeDtypeStruct(near_second.shape, near_second.dtype),
+            jax.ShapeDtypeStruct((4 * half, 112, 128), jnp.bfloat16),
+            jax.ShapeDtypeStruct((4 * half, 112, 128), jnp.bfloat16),
         ),
         in_specs=[vmem, anywhere, anywhere],
         out_specs=(vmem, vmem, vmem, anywhere, anywhere),
@@ -311,12 +320,12 @@
             pltpu.VMEM((STATIONS[stage] * 3, 48, 384), jnp.bfloat16),
             pltpu.VMEM((STATIONS[stage] * 3, 40, 128), jnp.float32),
             pltpu.VMEM((16 * 112, 128), jnp.float32),
-            pltpu.VMEM((16 * 112, 384), jnp.float32),
+            pltpu.VMEM((16 * 112, 256), jnp.float32),
             pltpu.SMEM((slots + 128,), jnp.int32),
             pltpu.SemaphoreType.DMA((PIECES[stage],)),
         ]
         result = pltpu.VMEM((total_rows, 32, 128), jnp.float32)
-        extra = jax.ShapeDtypeStruct((total_rows if stage == 2 else 1, 32, 128), jnp.bfloat16)
+        extra = jax.ShapeDtypeStruct((total_rows if stage == 3 else 1, 32, 128), jnp.bfloat16)
         carried = [pltpu.with_memory_space_constraint(p, pltpu.VMEM) for p in carried]
         return pl.pallas_call(
             functools.partial(pick_kernel, stage, per_source, taps),
@@ -325,7 +334,7 @@
             out_specs=(vmem, vmem),
             scratch_shapes=scratch,
             input_output_aliases={3 + PIECES[stage]: 0} if carried else {},
-            cost_estimate=pl.CostEstimate(flops=0, bytes_accessed=(30, 50, 30)[stage] * 10**6, transcendentals=0),
+            cost_estimate=pl.CostEstimate(flops=0, bytes_accessed=30 * 10**6, transcendentals=0),
             compiler_params=pltpu.CompilerParams(vmem_limit_bytes=48 * 2**20),
         )(marks, power, shapes, *gathered, *carried)
 
@@ -343,7 +352,8 @@
 
     far = ring(near_first, near_second, "z", after)
     partial, _ = run_stage(1, (far[0], far[3]), (partial,))
-    _, partial = run_stage(2, (far[1], far[2], far[4], far[5]), (partial,))
+    partial, _ = run_stage(2, (far[1], far[2]), (partial,))
+    _, partial = run_stage(3, (far[4], far[5]), (partial,))
 
     returned = lax.all_to_all(
         partial.reshape(columns, own_templates * 32, 128), "tpl", split_axis=0, concat_axis=0, tiled=True

time: 104 us -> 99.7 us (0.959); the launches traced: 104 us -> 98.3 us
  waiting for transfers between devices: 8.23 us -> 2.01 us
  Pallas kernels: 39.9 us -> 45.5 us
  blocking collectives: 29.8 us -> 26.5 us
  local copies, waits for them, and re-layouts: 1.77 us -> 0 us
    ppermute x2, waiting for transfers between devices: 7.57 us -> 1.14 us  [ring(): far_first = lax.ppermute(behind_first, 'sta', shifted(axis, 1))]
    pallas_call x3 -> x4, Pallas kernels: 34.8 us -> 40.4 us  [run_stage(): pl.pallas_call(functools.partial(pick_kernel, stage, per_source, taps), o...]
    all_to_all x1, blocking collectives: 29.8 us -> 26.5 us  [on_device(): lax.all_to_all(partial.reshape(columns, own_templates * 32, 128), 'tpl',...]
    ppermute x2, starting transfers between devices: 1.28 us -> 2.89 us  [ring(): behind_first = lax.ppermute(first, 'sta', shifted(axis, 1))]
    ppermute x2, starting transfers between devices: 5.27 us -> 3.67 us  [ring(): ahead_second = lax.ppermute(second, 'sta', shifted(axis, -1))]
    ppermute x2, starting transfers between devices: 5.38 us -> 4.06 us  [ring(): ahead_first = lax.ppermute(first, 'sta', shifted(axis, -1))]
    ppermute x2, starting transfers between devices: 5.34 us -> 6.38 us  [ring(): far_second = lax.ppermute(ahead_second, 'sta', shifted(axis, -1))]
  transfers between devices with their start and end apart: 13 -> 13, of which waited for: 3 -> 2; matrix products, arithmetic and copies ran while one was open for 2% -> 1% of each run, Pallas kernels for 18% -> 29%
where the time goes in v3:
time: 99.7 us; the launch traced here: 98.3 us
  Pallas kernels  45.5 us (46%)
  blocking collectives  26.5 us (27%)
  starting transfers between devices  23.1 us (23%)
  waiting for transfers between devices  2.01 us (2%)
  other arithmetic  1.07 us (1%)
    pallas_call x4, Pallas kernels, run_stage(): pl.pallas_call(functools.partial(pick_kernel, stage, per_source, taps), o...  40.4 us
    all_to_all x1, blocking collectives, on_device(): lax.all_to_all(partial.reshape(columns, own_templates * 32, 128), 'tpl',...  26.5 us
    ppermute x2, starting transfers between devices, ring(): far_second = lax.ppermute(ahead_second, 'sta', shifted(axis, -1))  6.38 us
    all_to_all x1, starting transfers between devices, on_device(): lax.all_to_all(outbox.reshape(columns, per_source, channels * 256), 'tpl'...  5.97 us
    ppermute x2, starting transfers between devices, ring(): ahead_first = lax.ppermute(first, 'sta', shifted(axis, -1))  4.06 us
    ppermute x2, starting transfers between devices, ring(): ahead_second = lax.ppermute(second, 'sta', shifted(axis, -1))  3.67 us
    pallas_call x1, Pallas kernels, on_device(): pl.pallas_call(functools.partial(front_kernel, per_source), out_shape=(ja...  3.26 us
    ppermute x2, starting transfers between devices, ring(): behind_first = lax.ppermute(first, 'sta', shifted(axis, 1))  2.89 us
  transfers between devices with their start and end apart: 13, of which 2 were waited for; matrix products, arithmetic and copies ran while one was open for 1% of the time, Pallas kernels for 29%

profile of v3, /device:TPU:1, one launch (start us, length us, event | category | flops | bytes accessed | tf_op | source)
XLA Modules:
  0.0 98.3 jit_solution(1123758436834035195)
XLA Ops:
  0.0 3.3 %shard_map.64 = (bf16[384,768]{1,0:T(8,128)(2,1)}, bf16[4,112,128]{2,1,0:T(8,128)(2,1)}, bf16[4,112,128]{2,1,0:T(8,128)(2,1)}) custom-call(s32[1]{0:T(128)} %bitcast.here, s32[10,24]{1,0:T(8,128)} %bitcast.16, s32[10,24]{1,0:T(8,128)} %bitcast.17, s32[10,24]{1,0:T(8,128)} %bitcast.18, s32[10,3,24]{2,1,0:T(4,128)} %bitcast.15, ...), custom_call_target="tpu_custom_call" | custom-call | tf_op jit(solution)/shard_map/pallas_call | solution.py:270
  3.3 6.0 %all-to-all-start = ((bf16[8,48,768]{2,1,0:T(8,128)(2,1)}), bf16[8,48,768]{2,1,0:T(8,128)(2,1)S(1)}, u32[]{:S(2)}, u32[]{:S(2)}) async-start(bf16[8,48,768]{2,1,0:T(8,128)(2,1)} %bitcast.12), calls=%async_computation | async-start | bytes 1179648 | tf_op jit(solution)/shard_map/all_to_all | solution.py:293
  9.2 1.2 %collective-permute-start = (bf16[4,112,128]{2,1,0:T(8,128)(2,1)}, bf16[4,112,128]{2,1,0:T(8,128)(2,1)S(1)}, u32[]{:S(2)}, u32[]{:S(2)}) collective-permute-start(bf16[4,112,128]{2,1,0:T(8,128)(2,1)} %get-tuple-element.21), channel_id=1, source_target_pairs={{0,32},{8,40},{16,48},{24,56},{32,64},{40,72},{48,80},{56,88},{64,... | collective-permute-start | bytes 344072 | tf_op jit(solution)/shard_map/ppermute | solution.py:31
  10.4 1.5 %collective-permute-start.3 = (bf16[4,112,128]{2,1,0:T(8,128)(2,1)}, bf16[4,112,128]{2,1,0:T(8,128)(2,1)S(1)}, u32[]{:S(2)}, u32[]{:S(2)}) collective-permute-start(bf16[4,112,128]{2,1,0:T(8,128)(2,1)} %get-tuple-element.22), channel_id=1, source_target_pairs={{0,96},{8,104},{16,112},{24,120},{32,0},{40,8},{48,16},{56,24},{64... | collective-permute-start | bytes 344072 | tf_op jit(solution)/shard_map/ppermute | solution.py:32
  11.9 0.0 collective-permute-start.1
  11.9 2.7 %collective-permute-start.2 = (bf16[4,112,128]{2,1,0:T(8,128)(2,1)}, bf16[4,112,128]{2,1,0:T(8,128)(2,1)S(1)}, u32[]{:S(2)}, u32[]{:S(2)}) collective-permute-start(bf16[4,112,128]{2,1,0:T(8,128)(2,1)} %get-tuple-element.21), channel_id=1, source_target_pairs={{0,96},{8,104},{16,112},{24,120},{32,0},{40,8},{48,16},{56,24},{64... | collective-permute-start | bytes 344072 | tf_op jit(solution)/shard_map/ppermute | solution.py:34
  14.6 0.8 collective-permute-done
  15.4 0.0 collective-permute-start.4
  15.4 0.0 collective-permute-done.3
  15.4 2.7 %collective-permute-start.5 = (bf16[4,112,128]{2,1,0:T(8,128)(2,1)S(1)}, bf16[4,112,128]{2,1,0:T(8,128)(2,1)S(1)}, u32[]{:S(2)}, u32[]{:S(2)}) collective-permute-start(bf16[4,112,128]{2,1,0:T(8,128)(2,1)S(1)} %collective-permute-done.3), channel_id=1, source_target_pairs={{0,96},{8,104},{16,112},{24,120},{32,0},{40,8},{48,16},{56,24},{64... | collective-permute-start | bytes 344072 | tf_op jit(solution)/shard_map/ppermute | solution.py:38
  18.1 0.0 collective-permute-done.1
  18.1 1.0 %pad_maximum_fusion.first = bf16[16,112,128]{2,1,0:T(8,128)(2,1)S(1)} fusion(bf16[4,112,128]{2,1,0:T(8,128)(2,1)S(1)} %collective-permute-done.1, bf16[4,112,128]{2,1,0:T(8,128)(2,1)S(1)} %collective-permute-done, bf16[4,112,128]{2,1,0:T(8,128)(2,1)} %get-tuple-element.22, bf16[4,112,128]{2,1,0:T(8,128)(2,1)} %get-tuple-element.21), kind=kLoop, calls=%fused_computation | loop fusion | flops 688128 | bytes 917504 | tf_op jit(solution)/shard_map/concatenate | solution.py:291
  19.1 0.0 collective-permute-done.2
  19.1 1.1 %collective-permute-done.4 = bf16[4,112,128]{2,1,0:T(8,128)(2,1)S(1)} collective-permute-done((bf16[4,112,128]{2,1,0:T(8,128)(2,1)S(1)}, bf16[4,112,128]{2,1,0:T(8,128)(2,1)S(1)}, u32[]{:S(2)}, u32[]{:S(2)}) %collective-permute-start.4) | collective-permute-done | bytes 114720 | tf_op jit(solution)/shard_map/ppermute | solution.py:37
  20.3 0.0 collective-permute-done.5
  20.3 0.1 pad_maximum_fusion.1.second
  20.4 0.0 all-to-all-done
  20.4 0.6 shard_map.65
  21.0 1.7 %collective-permute-start.6 = (bf16[16,112,128]{2,1,0:T(8,128)(2,1)S(1)}, bf16[16,112,128]{2,1,0:T(8,128)(2,1)S(1)}, u32[]{:S(2)}, u32[]{:S(2)}) collective-permute-start(bf16[16,112,128]{2,1,0:T(8,128)(2,1)S(1)} %get-tuple-element.26.refs_0_), channel_id=1, source_target_pairs={{0,8},{8,16},{16,24},{24,0},{32,40},{40,48},{48,56},{56,32},{64,72... | collective-permute-start | bytes 1376264 | tf_op jit(solution)/shard_map/ppermute | solution.py:31
  22.6 2.2 %collective-permute-start.7 = (bf16[16,112,128]{2,1,0:T(8,128)(2,1)S(1)}, bf16[16,112,128]{2,1,0:T(8,128)(2,1)S(1)}, u32[]{:S(2)}, u32[]{:S(2)}) collective-permute-start(bf16[16,112,128]{2,1,0:T(8,128)(2,1)S(1)} %get-tuple-element.27.refs_1_), channel_id=1, source_target_pairs={{0,24},{8,0},{16,8},{24,16},{32,56},{40,32},{48,40},{56,48},{64,88... | collective-permute-start | bytes 1376264 | tf_op jit(solution)/shard_map/ppermute | solution.py:32
  24.8 1.4 %collective-permute-start.11 = (bf16[16,112,128]{2,1,0:T(8,128)(2,1)S(1)}, bf16[16,112,128]{2,1,0:T(8,128)(2,1)S(1)}, u32[]{:S(2)}, u32[]{:S(2)}) collective-permute-start(bf16[16,112,128]{2,1,0:T(8,128)(2,1)S(1)} %get-tuple-element.26.refs_0_), channel_id=1, source_target_pairs={{0,24},{8,0},{16,8},{24,16},{32,56},{40,32},{48,40},{56,48},{64,88... | collective-permute-start | bytes 1376264 | tf_op jit(solution)/shard_map/ppermute | solution.py:34
  26.2 0.1 collective-permute-start.10
  26.3 9.0 %shard_map.66 = (f32[192,32,128]{2,1,0:T(8,128)S(1)}, bf16[1,32,128]{2,1,0:T(8,128)(2,1)S(1)}) custom-call(s32[16,512]{1,0:T(8,128)S(1)} %get-tuple-element.23.marks, f32[8,512]{1,0:T(8,128)S(1)} %get-tuple-element.24.power, f32[3080,128]{1,0:T(8,128)S(1)} %get-tuple-element.25.shapes, bf16[16,112,128]{2,1,0:T(8,128)(2,1)S(1)} %get-tuple-element.26.refs_0_, ...), custom_call_target="tpu_custom_call" | custom-call | bytes 30000000 | tf_op jit(solution)/shard_map/pallas_call | solution.py:330
  35.3 0.0 collective-permute-done.6.first
  35.3 0.0 collective-permute-done.7.second
  35.3 0.1 collective-permute-start.8
  35.4 3.7 %collective-permute-start.9 = (bf16[16,112,128]{2,1,0:T(8,128)(2,1)S(1)}, bf16[16,112,128]{2,1,0:T(8,128)(2,1)S(1)}, u32[]{:S(2)}, u32[]{:S(2)}) collective-permute-start(bf16[16,112,128]{2,1,0:T(8,128)(2,1)S(1)} %get-tuple-element.30.refs_1_), channel_id=1, source_target_pairs={{0,24},{8,0},{16,8},{24,16},{32,56},{40,32},{48,40},{56,48},{64,88... | collective-permute-start | bytes 1376264 | tf_op jit(solution)/shard_map/ppermute | solution.py:38
  39.1 10.6 %shard_map.68 = (f32[192,32,128]{2,1,0:T(8,128)S(1)}, bf16[1,32,128]{2,1,0:T(8,128)(2,1)}) custom-call(s32[16,512]{1,0:T(8,128)S(1)} %get-tuple-element.23.marks, f32[8,512]{1,0:T(8,128)S(1)} %get-tuple-element.24.power, f32[3080,128]{1,0:T(8,128)S(1)} %get-tuple-element.25.shapes, ...), custom_call_target="tpu_custom_call", output_to_operand_aliasing={{0}: (5, {})} | custom-call | bytes 30000000 | tf_op jit(solution)/shard_map/pallas_call | solution.py:330
  49.7 0.0 collective-permute-done.11.refs_1_
  49.7 0.0 collective-permute-done.10.refs_0_
  49.7 9.4 %shard_map.69 = (f32[192,32,128]{2,1,0:T(8,128)S(1)}, bf16[1,32,128]{2,1,0:T(8,128)(2,1)}) custom-call(s32[16,512]{1,0:T(8,128)S(1)} %get-tuple-element.23.marks, f32[8,512]{1,0:T(8,128)S(1)} %get-tuple-element.24.power, f32[3080,128]{1,0:T(8,128)S(1)} %get-tuple-element.25.shapes, ...), custom_call_target="tpu_custom_call", output_to_operand_aliasing={{0}: (5, {})} | custom-call | bytes 30000000 | tf_op jit(solution)/shard_map/pallas_call | solution.py:330
  59.1 0.0 collective-permute-done.8.refs_0_
  59.1 0.0 collective-permute-done.9.refs_1_
  59.1 11.4 %shard_map.70 = (f32[192,32,128]{2,1,0:T(8,128)S(1)}, bf16[192,32,128]{2,1,0:T(8,128)(2,1)}) custom-call(s32[16,512]{1,0:T(8,128)S(1)} %get-tuple-element.23.marks, f32[8,512]{1,0:T(8,128)S(1)} %get-tuple-element.24.power, f32[3080,128]{1,0:T(8,128)S(1)} %get-tuple-element.25.shapes, ...), custom_call_target="tpu_custom_call", output_to_operand_aliasing={{0}: (5, {})} | custom-call | bytes 30000000 | tf_op jit(solution)/shard_map/pallas_call | solution.py:330
  70.6 26.5 %all_to_all.10.parts = bf16[8,768,128]{2,1,0:T(8,128)(2,1)S(1)} all-to-all(bf16[8,768,128]{2,1,0:T(8,128)(2,1)} %bitcast.11), channel_id=1, replica_groups=mesh['sta'=16,'tpl'=8] {'tpl'}, dimensions={0} | all-to-all | bytes 3145728 | tf_op jit(solution)/shard_map/all_to_all | solution.py:358
  97.0 1.3 %shard_map.71 = f32[24,4096]{1,0:T(8,128)} custom-call(bf16[8,768,128]{2,1,0:T(8,128)(2,1)S(1)} %all_to_all.10.parts), custom_call_target="tpu_custom_call" | custom-call | tf_op jit(solution)/shard_map/pallas_call | solution.py:361
  (1 shorter events, 0.0 us)
Async XLA Ops:
  3.3 17.1 %all-to-all-start = ((bf16[8,48,768]{2,1,0:T(8,128)(2,1)}), bf16[8,48,768]{2,1,0:T(8,128)(2,1)S(1)}, u32[]{:S(2)}, u32[]{:S(2)}) async-start(bf16[8,48,768]{2,1,0:T(8,128)(2,1)} %bitcast.12), calls=%async_computation | async-start | bytes 1179648 | tf_op jit(solution)/shard_map/all_to_all | solution.py:293
  9.2 6.2 %collective-permute-start = (bf16[4,112,128]{2,1,0:T(8,128)(2,1)}, bf16[4,112,128]{2,1,0:T(8,128)(2,1)S(1)}, u32[]{:S(2)}, u32[]{:S(2)}) collective-permute-start(bf16[4,112,128]{2,1,0:T(8,128)(2,1)} %get-tuple-element.21), channel_id=1, source_target_pairs={{0,32},{8,40},{16,48},{24,56},{32,64},{40,72},{48,80},{56,88},{64,... | collective-permute-start | bytes 344072 | tf_op jit(solution)/shard_map/ppermute | solution.py:31
  10.4 5.0 %collective-permute-start.3 = (bf16[4,112,128]{2,1,0:T(8,128)(2,1)}, bf16[4,112,128]{2,1,0:T(8,128)(2,1)S(1)}, u32[]{:S(2)}, u32[]{:S(2)}) collective-permute-start(bf16[4,112,128]{2,1,0:T(8,128)(2,1)} %get-tuple-element.22), channel_id=1, source_target_pairs={{0,96},{8,104},{16,112},{24,120},{32,0},{40,8},{48,16},{56,24},{64... | collective-permute-start | bytes 344072 | tf_op jit(solution)/shard_map/ppermute | solution.py:32
  11.9 6.2 %collective-permute-start.1 = (bf16[4,112,128]{2,1,0:T(8,128)(2,1)}, bf16[4,112,128]{2,1,0:T(8,128)(2,1)S(1)}, u32[]{:S(2)}, u32[]{:S(2)}) collective-permute-start(bf16[4,112,128]{2,1,0:T(8,128)(2,1)} %get-tuple-element.22), channel_id=1, source_target_pairs={{0,32},{8,40},{16,48},{24,56},{32,64},{40,72},{48,80},{56,88},{64,... | collective-permute-start | bytes 344072 | tf_op jit(solution)/shard_map/ppermute | solution.py:33
  11.9 7.2 %collective-permute-start.2 = (bf16[4,112,128]{2,1,0:T(8,128)(2,1)}, bf16[4,112,128]{2,1,0:T(8,128)(2,1)S(1)}, u32[]{:S(2)}, u32[]{:S(2)}) collective-permute-start(bf16[4,112,128]{2,1,0:T(8,128)(2,1)} %get-tuple-element.21), channel_id=1, source_target_pairs={{0,96},{8,104},{16,112},{24,120},{32,0},{40,8},{48,16},{56,24},{64... | collective-permute-start | bytes 344072 | tf_op jit(solution)/shard_map/ppermute | solution.py:34
  15.4 4.9 %collective-permute-start.4 = (bf16[4,112,128]{2,1,0:T(8,128)(2,1)S(1)}, bf16[4,112,128]{2,1,0:T(8,128)(2,1)S(1)}, u32[]{:S(2)}, u32[]{:S(2)}) collective-permute-start(bf16[4,112,128]{2,1,0:T(8,128)(2,1)S(1)} %collective-permute-done), channel_id=1, source_target_pairs={{0,32},{8,40},{16,48},{24,56},{32,64},{40,72},{48,80},{56,88},{64,... | collective-permute-start | bytes 344072 | tf_op jit(solution)/shard_map/ppermute | solution.py:37
  15.4 4.8 %collective-permute-start.5 = (bf16[4,112,128]{2,1,0:T(8,128)(2,1)S(1)}, bf16[4,112,128]{2,1,0:T(8,128)(2,1)S(1)}, u32[]{:S(2)}, u32[]{:S(2)}) collective-permute-start(bf16[4,112,128]{2,1,0:T(8,128)(2,1)S(1)} %collective-permute-done.3), channel_id=1, source_target_pairs={{0,96},{8,104},{16,112},{24,120},{32,0},{40,8},{48,16},{56,24},{64... | collective-permute-start | bytes 344072 | tf_op jit(solution)/shard_map/ppermute | solution.py:38
  21.0 14.3 %collective-permute-start.6 = (bf16[16,112,128]{2,1,0:T(8,128)(2,1)S(1)}, bf16[16,112,128]{2,1,0:T(8,128)(2,1)S(1)}, u32[]{:S(2)}, u32[]{:S(2)}) collective-permute-start(bf16[16,112,128]{2,1,0:T(8,128)(2,1)S(1)} %get-tuple-element.26.refs_0_), channel_id=1, source_target_pairs={{0,8},{8,16},{16,24},{24,0},{32,40},{40,48},{48,56},{56,32},{64,72... | collective-permute-start | bytes 1376264 | tf_op jit(solution)/shard_map/ppermute | solution.py:31
  22.6 12.7 %collective-permute-start.7 = (bf16[16,112,128]{2,1,0:T(8,128)(2,1)S(1)}, bf16[16,112,128]{2,1,0:T(8,128)(2,1)S(1)}, u32[]{:S(2)}, u32[]{:S(2)}) collective-permute-start(bf16[16,112,128]{2,1,0:T(8,128)(2,1)S(1)} %get-tuple-element.27.refs_1_), channel_id=1, source_target_pairs={{0,24},{8,0},{16,8},{24,16},{32,56},{40,32},{48,40},{56,48},{64,88... | collective-permute-start | bytes 1376264 | tf_op jit(solution)/shard_map/ppermute | solution.py:32
  24.8 24.9 %collective-permute-start.11 = (bf16[16,112,128]{2,1,0:T(8,128)(2,1)S(1)}, bf16[16,112,128]{2,1,0:T(8,128)(2,1)S(1)}, u32[]{:S(2)}, u32[]{:S(2)}) collective-permute-start(bf16[16,112,128]{2,1,0:T(8,128)(2,1)S(1)} %get-tuple-element.26.refs_0_), channel_id=1, source_target_pairs={{0,24},{8,0},{16,8},{24,16},{32,56},{40,32},{48,40},{56,48},{64,88... | collective-permute-start | bytes 1376264 | tf_op jit(solution)/shard_map/ppermute | solution.py:34
  26.2 23.5 %collective-permute-start.10 = (bf16[16,112,128]{2,1,0:T(8,128)(2,1)S(1)}, bf16[16,112,128]{2,1,0:T(8,128)(2,1)S(1)}, u32[]{:S(2)}, u32[]{:S(2)}) collective-permute-start(bf16[16,112,128]{2,1,0:T(8,128)(2,1)S(1)} %get-tuple-element.27.refs_1_), channel_id=1, source_target_pairs={{0,8},{8,16},{16,24},{24,0},{32,40},{40,48},{48,56},{56,32},{64,72... | collective-permute-start | bytes 1376264 | tf_op jit(solution)/shard_map/ppermute | solution.py:33
  35.3 23.8 %collective-permute-start.8 = (bf16[16,112,128]{2,1,0:T(8,128)(2,1)S(1)}, bf16[16,112,128]{2,1,0:T(8,128)(2,1)S(1)}, u32[]{:S(2)}, u32[]{:S(2)}) collective-permute-start(bf16[16,112,128]{2,1,0:T(8,128)(2,1)S(1)} %get-tuple-element.29.refs_0_), channel_id=1, source_target_pairs={{0,8},{8,16},{16,24},{24,0},{32,40},{40,48},{48,56},{56,32},{64,72... | collective-permute-start | bytes 1376264 | tf_op jit(solution)/shard_map/ppermute | solution.py:37
  35.4 23.7 %collective-permute-start.9 = (bf16[16,112,128]{2,1,0:T(8,128)(2,1)S(1)}, bf16[16,112,128]{2,1,0:T(8,128)(2,1)S(1)}, u32[]{:S(2)}, u32[]{:S(2)}) collective-permute-start(bf16[16,112,128]{2,1,0:T(8,128)(2,1)S(1)} %get-tuple-element.30.refs_1_), channel_id=1, source_target_pairs={{0,24},{8,0},{16,8},{24,16},{32,56},{40,32},{48,40},{56,48},{64,88... | collective-permute-start | bytes 1376264 | tf_op jit(solution)/shard_map/ppermute | solution.py:38

commit v4 on v3

--- a/solution.py
+++ b/solution.py
@@ -127,12 +127,13 @@
     power[:, slots : slots + 128] = jnp.zeros((8, 128), jnp.float32)
 
 
-def pick_kernel(stage, per_source, taps, marks, power, shapes, *refs):
+def pick_kernel(stage, per_source, taps, here, marks, power, shapes, *refs):
     pieces = refs[: PIECES[stage]]
     refs = refs[PIECES[stage] :]
     if stage > 0:
         refs = refs[1:]
-    total, extra, records, frames, energy, wide, sums, order, sem = refs
+    total, extras = refs[0], refs[1:-7]
+    records, frames, energy, wide, sums, order, sem = refs[-7:]
     copies = []
     base = 0
     for number, piece in enumerate(pieces):
@@ -239,15 +240,18 @@
         return carry
 
     lax.fori_loop(whole * (UNROLL // 4), (taken + 3) // 4, rest, 0)
-    extra[...] = total[: extra.shape[0]].astype(extra.dtype)
-
-
-def stack_kernel(parts, out, total):
+    for step, extra in enumerate(extras):
+        rows = extra.shape[0]
+        target = (here[0] + step) & 7 if stage == len(PIECES) - 1 else 0
+        extra[...] = total[pl.ds(target * rows, rows)].astype(extra.dtype)
+
+
+def stack_kernel(*refs):
+    parts, (out, total) = refs[:-2], refs[-2:]
     rows = out.shape[0]
-    summed = parts[0].astype(jnp.float32)
-    for p in range(1, parts.shape[0]):
-        summed = summed + parts[p].astype(jnp.float32)
-    cube = summed.reshape(rows, 32, 128)
+    cube = parts[0][...].astype(jnp.float32)
+    for part in parts[1:]:
+        cube = cube + part[...].astype(jnp.float32)
     square = jnp.sum(jnp.sum(cube * cube, axis=2, keepdims=True), axis=1, keepdims=True)
     level = jnp.sqrt(square / (32 * 128) + EPS)
     total[...] = (cube / level).reshape(rows * 32, 128)
@@ -314,6 +318,8 @@
     )(inbox.reshape(slots, channels * 256), near_first, near_second)
     shapes = pltpu.with_memory_space_constraint(shapes, pltpu.VMEM)
 
+    place = lax.axis_index("tpl").astype(jnp.int32).reshape(1)
+
     def run_stage(stage, gathered, carried):
         scratch = [
             pltpu.VMEM((STATIONS[stage], 112, 128), jnp.bfloat16),
@@ -325,18 +331,21 @@
             pltpu.SemaphoreType.DMA((PIECES[stage],)),
         ]
         result = pltpu.VMEM((total_rows, 32, 128), jnp.float32)
-        extra = jax.ShapeDtypeStruct((total_rows if stage == 3 else 1, 32, 128), jnp.bfloat16)
+        if stage == len(PIECES) - 1:
+            extras = (jax.ShapeDtypeStruct((own_templates, 32, 128), jnp.bfloat16),) * columns
+        else:
+            extras = (jax.ShapeDtypeStruct((1, 32, 128), jnp.bfloat16),)
         carried = [pltpu.with_memory_space_constraint(p, pltpu.VMEM) for p in carried]
         return pl.pallas_call(
             functools.partial(pick_kernel, stage, per_source, taps),
-            out_shape=(result, extra),
-            in_specs=[smem, smem, vmem] + [anywhere] * PIECES[stage] + [vmem] * len(carried),
-            out_specs=(vmem, vmem),
+            out_shape=(result,) + extras,
+            in_specs=[smem, smem, smem, vmem] + [anywhere] * PIECES[stage] + [vmem] * len(carried),
+            out_specs=(vmem,) * (1 + len(extras)),
             scratch_shapes=scratch,
-            input_output_aliases={3 + PIECES[stage]: 0} if carried else {},
+            input_output_aliases={4 + PIECES[stage]: 0} if carried else {},
             cost_estimate=pl.CostEstimate(flops=0, bytes_accessed=30 * 10**6, transcendentals=0),
             compiler_params=pltpu.CompilerParams(vmem_limit_bytes=48 * 2**20),
-        )(marks, power, shapes, *gathered, *carried)
+        )(place, marks, power, shapes, *gathered, *carried)
 
     partial, token = run_stage(0, (near_first, near_second), ())
 
@@ -353,19 +362,20 @@
     far = ring(near_first, near_second, "z", after)
     partial, _ = run_stage(1, (far[0], far[3]), (partial,))
     partial, _ = run_stage(2, (far[1], far[2]), (partial,))
-    _, partial = run_stage(3, (far[4], far[5]), (partial,))
-
-    returned = lax.all_to_all(
-        partial.reshape(columns, own_templates * 32, 128), "tpl", split_axis=0, concat_axis=0, tiled=True
-    )
+    _, *partial = run_stage(3, (far[4], far[5]), (partial,))
+
+    returned = [
+        lax.ppermute(part, "tpl", [(i, (i + step) % columns) for i in range(columns)]) if step else part
+        for step, part in enumerate(partial)
+    ]
     return pl.pallas_call(
         stack_kernel,
         out_shape=jax.ShapeDtypeStruct((own_templates, 4096), jnp.float32),
-        in_specs=[vmem],
+        in_specs=[vmem] * columns,
         out_specs=vmem,
         scratch_shapes=[pltpu.VMEM((own_templates * 32, 128), jnp.float32)],
         compiler_params=pltpu.CompilerParams(vmem_limit_bytes=20 * 2**20),
-    )(returned)
+    )(*returned)
 
 
 def solution(mesh):

time: 99.7 us -> 97.2 us (0.975); the launches traced: 98.3 us -> 97.5 us
  blocking collectives: 26.5 us -> 0 us
  waiting for transfers between devices: 2.01 us -> 16.1 us
  starting transfers between devices: 23.1 us -> 35.8 us
  Pallas kernels: 45.5 us -> 43.5 us
    all_to_all x1 -> x0, blocking collectives: 26.5 us -> none  [on_device(): lax.all_to_all(partial.reshape(columns, own_templates * 32, 128), 'tpl',...]
    ppermute x0 -> x7, waiting for transfers between devices: none -> 14.1 us  [on_device(): lax.ppermute(part, 'tpl', [(i, (i + step) % columns) for i in range(colum...]
    ppermute x0 -> x7, starting transfers between devices: none -> 13.7 us  [on_device(): lax.ppermute(part, 'tpl', [(i, (i + step) % columns) for i in range(colum...]
    ppermute x2, starting transfers between devices: 6.38 us -> 4.3 us  [ring(): far_second = lax.ppermute(ahead_second, 'sta', shifted(axis, -1))]
    pallas_call x4, Pallas kernels: 40.4 us -> 38.4 us  [run_stage(): pl.pallas_call(functools.partial(pick_kernel, stage, per_source, taps), o...]
    ppermute x2, starting transfers between devices: 0.08 us -> 1.13 us  [ring(): far_first = lax.ppermute(behind_first, 'sta', shifted(axis, 1))]
  transfers between devices with their start and end apart: 13 -> 20, of which waited for: 2 -> 6; matrix products, arithmetic and copies ran while one was open for 1% -> 1% of each run, Pallas kernels for 29% -> 30%
where the time goes in v4:
time: 97.2 us; the launch traced here: 97.5 us
  Pallas kernels  43.5 us (45%)
  starting transfers between devices  35.8 us (37%)
  waiting for transfers between devices  16.1 us (17%)
  other arithmetic  1.07 us (1%)
    pallas_call x4, Pallas kernels, run_stage(): pl.pallas_call(functools.partial(pick_kernel, stage, per_source, taps), o...  38.4 us
    ppermute x7, waiting for transfers between devices, on_device(): lax.ppermute(part, 'tpl', [(i, (i + step) % columns) for i in range(colum...  14.1 us
    ppermute x7, starting transfers between devices, on_device(): lax.ppermute(part, 'tpl', [(i, (i + step) % columns) for i in range(colum...  13.7 us
    all_to_all x1, starting transfers between devices, on_device(): lax.all_to_all(outbox.reshape(columns, per_source, channels * 256), 'tpl'...  5.97 us
    ppermute x2, starting transfers between devices, ring(): far_second = lax.ppermute(ahead_second, 'sta', shifted(axis, -1))  4.3 us
    ppermute x2, starting transfers between devices, ring(): ahead_first = lax.ppermute(first, 'sta', shifted(axis, -1))  4.06 us
    ppermute x2, starting transfers between devices, ring(): ahead_second = lax.ppermute(second, 'sta', shifted(axis, -1))  3.67 us
    pallas_call x1, Pallas kernels, on_device(): pl.pallas_call(functools.partial(front_kernel, per_source), out_shape=(ja...  3.26 us
  transfers between devices with their start and end apart: 20, of which 6 were waited for; matrix products, arithmetic and copies ran while one was open for 1% of the time, Pallas kernels for 30%

profile of v4, /device:TPU:1, one launch (start us, length us, event | category | flops | bytes accessed | tf_op | source)
XLA Modules:
  0.0 97.5 jit_solution(7962297663197506297)
XLA Ops:
  0.0 3.3 %shard_map.64 = (bf16[384,768]{1,0:T(8,128)(2,1)}, bf16[4,112,128]{2,1,0:T(8,128)(2,1)}, bf16[4,112,128]{2,1,0:T(8,128)(2,1)}) custom-call(s32[1]{0:T(128)} %bitcast.1.here, s32[10,24]{1,0:T(8,128)} %bitcast.15, s32[10,24]{1,0:T(8,128)} %bitcast.16, s32[10,24]{1,0:T(8,128)} %bitcast.17, s32[10,3,24]{2,1,0:T(4,128)} %bitcast.14, ...), custom_call_target="tpu_custom_call" | custom-call | tf_op jit(solution)/shard_map/pallas_call | solution.py:274
  3.3 6.0 %all-to-all-start = ((bf16[8,48,768]{2,1,0:T(8,128)(2,1)}), bf16[8,48,768]{2,1,0:T(8,128)(2,1)S(1)}, u32[]{:S(2)}, u32[]{:S(2)}) async-start(bf16[8,48,768]{2,1,0:T(8,128)(2,1)} %bitcast.11), calls=%async_computation | async-start | bytes 1179648 | tf_op jit(solution)/shard_map/all_to_all | solution.py:297
  9.2 1.2 %collective-permute-start = (bf16[4,112,128]{2,1,0:T(8,128)(2,1)}, bf16[4,112,128]{2,1,0:T(8,128)(2,1)S(1)}, u32[]{:S(2)}, u32[]{:S(2)}) collective-permute-start(bf16[4,112,128]{2,1,0:T(8,128)(2,1)} %get-tuple-element.28), channel_id=1, source_target_pairs={{0,32},{8,40},{16,48},{24,56},{32,64},{40,72},{48,80},{56,88},{64,... | collective-permute-start | bytes 344072 | tf_op jit(solution)/shard_map/ppermute | solution.py:31
  10.4 1.5 %collective-permute-start.3 = (bf16[4,112,128]{2,1,0:T(8,128)(2,1)}, bf16[4,112,128]{2,1,0:T(8,128)(2,1)S(1)}, u32[]{:S(2)}, u32[]{:S(2)}) collective-permute-start(bf16[4,112,128]{2,1,0:T(8,128)(2,1)} %get-tuple-element.29), channel_id=1, source_target_pairs={{0,96},{8,104},{16,112},{24,120},{32,0},{40,8},{48,16},{56,24},{64... | collective-permute-start | bytes 344072 | tf_op jit(solution)/shard_map/ppermute | solution.py:32
  11.9 0.0 collective-permute-start.1
  11.9 2.7 %collective-permute-start.2 = (bf16[4,112,128]{2,1,0:T(8,128)(2,1)}, bf16[4,112,128]{2,1,0:T(8,128)(2,1)S(1)}, u32[]{:S(2)}, u32[]{:S(2)}) collective-permute-start(bf16[4,112,128]{2,1,0:T(8,128)(2,1)} %get-tuple-element.28), channel_id=1, source_target_pairs={{0,96},{8,104},{16,112},{24,120},{32,0},{40,8},{48,16},{56,24},{64... | collective-permute-start | bytes 344072 | tf_op jit(solution)/shard_map/ppermute | solution.py:34
  14.6 0.8 collective-permute-done
  15.4 0.0 collective-permute-start.4
  15.4 0.0 collective-permute-done.3
  15.4 2.7 %collective-permute-start.5 = (bf16[4,112,128]{2,1,0:T(8,128)(2,1)S(1)}, bf16[4,112,128]{2,1,0:T(8,128)(2,1)S(1)}, u32[]{:S(2)}, u32[]{:S(2)}) collective-permute-start(bf16[4,112,128]{2,1,0:T(8,128)(2,1)S(1)} %collective-permute-done.3), channel_id=1, source_target_pairs={{0,96},{8,104},{16,112},{24,120},{32,0},{40,8},{48,16},{56,24},{64... | collective-permute-start | bytes 344072 | tf_op jit(solution)/shard_map/ppermute | solution.py:38
  18.1 0.0 collective-permute-done.1
  18.1 1.0 %pad_maximum_fusion.first = bf16[16,112,128]{2,1,0:T(8,128)(2,1)S(1)} fusion(bf16[4,112,128]{2,1,0:T(8,128)(2,1)S(1)} %collective-permute-done.1, bf16[4,112,128]{2,1,0:T(8,128)(2,1)S(1)} %collective-permute-done, bf16[4,112,128]{2,1,0:T(8,128)(2,1)} %get-tuple-element.29, bf16[4,112,128]{2,1,0:T(8,128)(2,1)} %get-tuple-element.28), kind=kLoop, calls=%fused_computation | loop fusion | flops 688128 | bytes 917504 | tf_op jit(solution)/shard_map/concatenate | solution.py:295
  19.1 0.0 collective-permute-done.2
  19.1 1.1 %collective-permute-done.4 = bf16[4,112,128]{2,1,0:T(8,128)(2,1)S(1)} collective-permute-done((bf16[4,112,128]{2,1,0:T(8,128)(2,1)S(1)}, bf16[4,112,128]{2,1,0:T(8,128)(2,1)S(1)}, u32[]{:S(2)}, u32[]{:S(2)}) %collective-permute-start.4) | collective-permute-done | bytes 114720 | tf_op jit(solution)/shard_map/ppermute | solution.py:37
  20.3 0.0 collective-permute-done.5
  20.3 0.1 pad_maximum_fusion.1.second
  20.4 0.0 all-to-all-done
  20.4 0.6 shard_map.65
  21.0 1.7 %collective-permute-start.6 = (bf16[16,112,128]{2,1,0:T(8,128)(2,1)S(1)}, bf16[16,112,128]{2,1,0:T(8,128)(2,1)S(1)}, u32[]{:S(2)}, u32[]{:S(2)}) collective-permute-start(bf16[16,112,128]{2,1,0:T(8,128)(2,1)S(1)} %get-tuple-element.33.refs_0_), channel_id=1, source_target_pairs={{0,8},{8,16},{16,24},{24,0},{32,40},{40,48},{48,56},{56,32},{64,72... | collective-permute-start | bytes 1376264 | tf_op jit(solution)/shard_map/ppermute | solution.py:31
  22.6 2.2 %collective-permute-start.7 = (bf16[16,112,128]{2,1,0:T(8,128)(2,1)S(1)}, bf16[16,112,128]{2,1,0:T(8,128)(2,1)S(1)}, u32[]{:S(2)}, u32[]{:S(2)}) collective-permute-start(bf16[16,112,128]{2,1,0:T(8,128)(2,1)S(1)} %get-tuple-element.34.refs_1_), channel_id=1, source_target_pairs={{0,24},{8,0},{16,8},{24,16},{32,56},{40,32},{48,40},{56,48},{64,88... | collective-permute-start | bytes 1376264 | tf_op jit(solution)/shard_map/ppermute | solution.py:32
  24.8 1.4 %collective-permute-start.11 = (bf16[16,112,128]{2,1,0:T(8,128)(2,1)S(1)}, bf16[16,112,128]{2,1,0:T(8,128)(2,1)S(1)}, u32[]{:S(2)}, u32[]{:S(2)}) collective-permute-start(bf16[16,112,128]{2,1,0:T(8,128)(2,1)S(1)} %get-tuple-element.33.refs_0_), channel_id=1, source_target_pairs={{0,24},{8,0},{16,8},{24,16},{32,56},{40,32},{48,40},{56,48},{64,88... | collective-permute-start | bytes 1376264 | tf_op jit(solution)/shard_map/ppermute | solution.py:34
  26.2 0.1 collective-permute-start.10
  26.3 9.2 %shard_map.66 = (f32[192,32,128]{2,1,0:T(8,128)S(1)}, bf16[1,32,128]{2,1,0:T(8,128)(2,1)S(1)}) custom-call(s32[1]{0:T(128)} %bitcast.here, s32[16,512]{1,0:T(8,128)S(1)} %get-tuple-element.30.marks, f32[8,512]{1,0:T(8,128)S(1)} %get-tuple-element.31.power, f32[3080,128]{1,0:T(8,128)S(1)} %get-tuple-element.32.shapes, ...), custom_call_target="tpu_custom_call" | custom-call | bytes 30000000 | tf_op jit(solution)/shard_map/pallas_call | solution.py:339
  35.5 0.0 collective-permute-done.6.first
  35.5 0.0 collective-permute-done.7.second
  35.6 1.1 %collective-permute-start.8 = (bf16[16,112,128]{2,1,0:T(8,128)(2,1)S(1)}, bf16[16,112,128]{2,1,0:T(8,128)(2,1)S(1)}, u32[]{:S(2)}, u32[]{:S(2)}) collective-permute-start(bf16[16,112,128]{2,1,0:T(8,128)(2,1)S(1)} %get-tuple-element.36.refs_0_), channel_id=1, source_target_pairs={{0,8},{8,16},{16,24},{24,0},{32,40},{40,48},{48,56},{56,32},{64,72... | collective-permute-start | bytes 1376264 | tf_op jit(solution)/shard_map/ppermute | solution.py:37
  36.7 1.6 %collective-permute-start.9 = (bf16[16,112,128]{2,1,0:T(8,128)(2,1)S(1)}, bf16[16,112,128]{2,1,0:T(8,128)(2,1)S(1)}, u32[]{:S(2)}, u32[]{:S(2)}) collective-permute-start(bf16[16,112,128]{2,1,0:T(8,128)(2,1)S(1)} %get-tuple-element.37.refs_1_), channel_id=1, source_target_pairs={{0,24},{8,0},{16,8},{24,16},{32,56},{40,32},{48,40},{56,48},{64,88... | collective-permute-start | bytes 1376264 | tf_op jit(solution)/shard_map/ppermute | solution.py:38
  38.3 10.8 %shard_map.68 = (f32[192,32,128]{2,1,0:T(8,128)S(1)}, bf16[1,32,128]{2,1,0:T(8,128)(2,1)}) custom-call(s32[1]{0:T(128)} %bitcast.here, s32[16,512]{1,0:T(8,128)S(1)} %get-tuple-element.30.marks, f32[8,512]{1,0:T(8,128)S(1)} %get-tuple-element.31.power, f32[3080,128]{1,0:T(8,128)S(1)} %get-tuple-element.32.shapes, ...), custom_call_target="tpu_custom_call", output_to_operand_aliasing={{0}: (6, {})} | custom-call | bytes 30000000 | tf_op jit(solution)/shard_map/pallas_call | solution.py:339
  49.2 0.0 collective-permute-done.11.refs_1_
  49.2 0.0 collective-permute-done.10.refs_0_
  49.2 9.6 %shard_map.69 = (f32[192,32,128]{2,1,0:T(8,128)S(1)}, bf16[1,32,128]{2,1,0:T(8,128)(2,1)}) custom-call(s32[1]{0:T(128)} %bitcast.here, s32[16,512]{1,0:T(8,128)S(1)} %get-tuple-element.30.marks, f32[8,512]{1,0:T(8,128)S(1)} %get-tuple-element.31.power, f32[3080,128]{1,0:T(8,128)S(1)} %get-tuple-element.32.shapes, ...), custom_call_target="tpu_custom_call", output_to_operand_aliasing={{0}: (6, {})} | custom-call | bytes 30000000 | tf_op jit(solution)/shard_map/pallas_call | solution.py:339
  58.8 0.0 collective-permute-done.8.refs_0_
  58.8 0.0 copy-start
  58.9 0.0 collective-permute-done.9.refs_1_
  58.9 0.0 copy-start.1
  58.9 0.7 copy-done
  59.6 0.2 copy-done.1
  59.8 8.7 %shard_map.70 = (f32[192,32,128]{2,1,0:T(8,128)S(1)}, bf16[24,32,128]{2,1,0:T(8,128)(2,1)S(1)}, bf16[24,32,128]{2,1,0:T(8,128)(2,1)S(1)}, bf16[24,32,128]{2,1,0:...) custom-call(s32[1]{0:T(128)} %bitcast.here, ...), custom_call_target="tpu_custom_call", output_to_operand_aliasing={{0}: (6, {})} | custom-call | bytes 30000000 | tf_op jit(solution)/shard_map/pallas_call | solution.py:339
  68.4 3.6 %collective-permute-start.12 = (bf16[24,32,128]{2,1,0:T(8,128)(2,1)S(1)}, bf16[24,32,128]{2,1,0:T(8,128)(2,1)S(1)}, u32[]{:S(2)}, u32[]{:S(2)}) collective-permute-start(bf16[24,32,128]{2,1,0:T(8,128)(2,1)S(1)} %get-tuple-element.42), channel_id=1, source_target_pairs={{0,1},{1,2},{2,3},{3,4},{4,5},{5,6},{6,7},{7,0},{8,9},{9,10},{10,1... | collective-permute-start | bytes 589832 | tf_op jit(solution)/shard_map/ppermute | solution.py:368
  72.0 1.3 %collective-permute-start.13 = (bf16[24,32,128]{2,1,0:T(8,128)(2,1)S(1)}, bf16[24,32,128]{2,1,0:T(8,128)(2,1)S(1)}, u32[]{:S(2)}, u32[]{:S(2)}) collective-permute-start(bf16[24,32,128]{2,1,0:T(8,128)(2,1)S(1)} %get-tuple-element.43), channel_id=1, source_target_pairs={{0,2},{1,3},{2,4},{3,5},{4,6},{5,7},{6,0},{7,1},{8,10},{9,11},{10,... | collective-permute-start | bytes 589832 | tf_op jit(solution)/shard_map/ppermute | solution.py:368
  73.3 5.5 %collective-permute-start.14 = (bf16[24,32,128]{2,1,0:T(8,128)(2,1)S(1)}, bf16[24,32,128]{2,1,0:T(8,128)(2,1)S(1)}, u32[]{:S(2)}, u32[]{:S(2)}) collective-permute-start(bf16[24,32,128]{2,1,0:T(8,128)(2,1)S(1)} %get-tuple-element.44), channel_id=1, source_target_pairs={{0,3},{1,4},{2,5},{3,6},{4,7},{5,0},{6,1},{7,2},{8,11},{9,12},{10,... | collective-permute-start | bytes 589832 | tf_op jit(solution)/shard_map/ppermute | solution.py:368
  78.8 0.0 collective-permute-start.15
  78.8 2.3 %collective-permute-start.16 = (bf16[24,32,128]{2,1,0:T(8,128)(2,1)S(1)}, bf16[24,32,128]{2,1,0:T(8,128)(2,1)S(1)}, u32[]{:S(2)}, u32[]{:S(2)}) collective-permute-start(bf16[24,32,128]{2,1,0:T(8,128)(2,1)S(1)} %get-tuple-element.46), channel_id=1, source_target_pairs={{0,5},{1,6},{2,7},{3,0},{4,1},{5,2},{6,3},{7,4},{8,13},{9,14},{10,... | collective-permute-start | bytes 589832 | tf_op jit(solution)/shard_map/ppermute | solution.py:368
  81.1 0.0 collective-permute-done.12.refs_1_
  81.1 0.8 collective-permute-start.17
  81.9 2.1 %collective-permute-done.13.refs_2_ = bf16[24,32,128]{2,1,0:T(8,128)(2,1)S(1)} collective-permute-done((bf16[24,32,128]{2,1,0:T(8,128)(2,1)S(1)}, bf16[24,32,128]{2,1,0:T(8,128)(2,1)S(1)}, u32[]{:S(2)}, u32[]{:S(2)}) %collective-permute-start.13) | collective-permute-done | bytes 196640 | tf_op jit(solution)/shard_map/ppermute | solution.py:368
  84.0 0.2 collective-permute-start.18
  84.2 1.3 %collective-permute-done.14.refs_3_ = bf16[24,32,128]{2,1,0:T(8,128)(2,1)S(1)} collective-permute-done((bf16[24,32,128]{2,1,0:T(8,128)(2,1)S(1)}, bf16[24,32,128]{2,1,0:T(8,128)(2,1)S(1)}, u32[]{:S(2)}, u32[]{:S(2)}) %collective-permute-start.14) | collective-permute-done | bytes 196640 | tf_op jit(solution)/shard_map/ppermute | solution.py:368
  85.5 10.1 %collective-permute-done.15.refs_4_ = bf16[24,32,128]{2,1,0:T(8,128)(2,1)S(1)} collective-permute-done((bf16[24,32,128]{2,1,0:T(8,128)(2,1)S(1)}, bf16[24,32,128]{2,1,0:T(8,128)(2,1)S(1)}, u32[]{:S(2)}, u32[]{:S(2)}) %collective-permute-start.15) | collective-permute-done | bytes 196640 | tf_op jit(solution)/shard_map/ppermute | solution.py:368
  95.6 0.6 collective-permute-done.16.refs_5_
  96.2 0.0 collective-permute-done.17.refs_6_
  96.2 0.0 collective-permute-done.18.refs_7_
  96.2 1.3 %shard_map.71 = f32[24,4096]{1,0:T(8,128)} custom-call(bf16[24,32,128]{2,1,0:T(8,128)(2,1)S(1)} %get-tuple-element.41.refs_0_, bf16[24,32,128]{2,1,0:T(8,128)(2,1)S(1)} %collective-permute-done.12.refs_1_, bf16[24,32,128]{2,1,0:T(8,128)(2,1)S(1)} %collective-permute-done.13.refs_2_, bf16[24,32,128]{2,1,0:T(8,128)(2,1)S(1)} %collective-permute-done.14.refs_3_, ...), custom_call_target="tpu_custom_call" | custom-call | tf_op jit(solution)/shard_map/pallas_call | solution.py:371
  (1 shorter events, 0.0 us)
Async XLA Ops:
  3.3 17.1 %all-to-all-start = ((bf16[8,48,768]{2,1,0:T(8,128)(2,1)}), bf16[8,48,768]{2,1,0:T(8,128)(2,1)S(1)}, u32[]{:S(2)}, u32[]{:S(2)}) async-start(bf16[8,48,768]{2,1,0:T(8,128)(2,1)} %bitcast.11), calls=%async_computation | async-start | bytes 1179648 | tf_op jit(solution)/shard_map/all_to_all | solution.py:297
  9.2 6.2 %collective-permute-start = (bf16[4,112,128]{2,1,0:T(8,128)(2,1)}, bf16[4,112,128]{2,1,0:T(8,128)(2,1)S(1)}, u32[]{:S(2)}, u32[]{:S(2)}) collective-permute-start(bf16[4,112,128]{2,1,0:T(8,128)(2,1)} %get-tuple-element.28), channel_id=1, source_target_pairs={{0,32},{8,40},{16,48},{24,56},{32,64},{40,72},{48,80},{56,88},{64,... | collective-permute-start | bytes 344072 | tf_op jit(solution)/shard_map/ppermute | solution.py:31
  10.4 5.0 %collective-permute-start.3 = (bf16[4,112,128]{2,1,0:T(8,128)(2,1)}, bf16[4,112,128]{2,1,0:T(8,128)(2,1)S(1)}, u32[]{:S(2)}, u32[]{:S(2)}) collective-permute-start(bf16[4,112,128]{2,1,0:T(8,128)(2,1)} %get-tuple-element.29), channel_id=1, source_target_pairs={{0,96},{8,104},{16,112},{24,120},{32,0},{40,8},{48,16},{56,24},{64... | collective-permute-start | bytes 344072 | tf_op jit(solution)/shard_map/ppermute | solution.py:32
  11.9 6.2 %collective-permute-start.1 = (bf16[4,112,128]{2,1,0:T(8,128)(2,1)}, bf16[4,112,128]{2,1,0:T(8,128)(2,1)S(1)}, u32[]{:S(2)}, u32[]{:S(2)}) collective-permute-start(bf16[4,112,128]{2,1,0:T(8,128)(2,1)} %get-tuple-element.29), channel_id=1, source_target_pairs={{0,32},{8,40},{16,48},{24,56},{32,64},{40,72},{48,80},{56,88},{64,... | collective-permute-start | bytes 344072 | tf_op jit(solution)/shard_map/ppermute | solution.py:33
  11.9 7.2 %collective-permute-start.2 = (bf16[4,112,128]{2,1,0:T(8,128)(2,1)}, bf16[4,112,128]{2,1,0:T(8,128)(2,1)S(1)}, u32[]{:S(2)}, u32[]{:S(2)}) collective-permute-start(bf16[4,112,128]{2,1,0:T(8,128)(2,1)} %get-tuple-element.28), channel_id=1, source_target_pairs={{0,96},{8,104},{16,112},{24,120},{32,0},{40,8},{48,16},{56,24},{64... | collective-permute-start | bytes 344072 | tf_op jit(solution)/shard_map/ppermute | solution.py:34
  15.4 4.9 %collective-permute-start.4 = (bf16[4,112,128]{2,1,0:T(8,128)(2,1)S(1)}, bf16[4,112,128]{2,1,0:T(8,128)(2,1)S(1)}, u32[]{:S(2)}, u32[]{:S(2)}) collective-permute-start(bf16[4,112,128]{2,1,0:T(8,128)(2,1)S(1)} %collective-permute-done), channel_id=1, source_target_pairs={{0,32},{8,40},{16,48},{24,56},{32,64},{40,72},{48,80},{56,88},{64,... | collective-permute-start | bytes 344072 | tf_op jit(solution)/shard_map/ppermute | solution.py:37
  15.4 4.8 %collective-permute-start.5 = (bf16[4,112,128]{2,1,0:T(8,128)(2,1)S(1)}, bf16[4,112,128]{2,1,0:T(8,128)(2,1)S(1)}, u32[]{:S(2)}, u32[]{:S(2)}) collective-permute-start(bf16[4,112,128]{2,1,0:T(8,128)(2,1)S(1)} %collective-permute-done.3), channel_id=1, source_target_pairs={{0,96},{8,104},{16,112},{24,120},{32,0},{40,8},{48,16},{56,24},{64... | collective-permute-start | bytes 344072 | tf_op jit(solution)/shard_map/ppermute | solution.py:38
  21.0 14.6 %collective-permute-start.6 = (bf16[16,112,128]{2,1,0:T(8,128)(2,1)S(1)}, bf16[16,112,128]{2,1,0:T(8,128)(2,1)S(1)}, u32[]{:S(2)}, u32[]{:S(2)}) collective-permute-start(bf16[16,112,128]{2,1,0:T(8,128)(2,1)S(1)} %get-tuple-element.33.refs_0_), channel_id=1, source_target_pairs={{0,8},{8,16},{16,24},{24,0},{32,40},{40,48},{48,56},{56,32},{64,72... | collective-permute-start | bytes 1376264 | tf_op jit(solution)/shard_map/ppermute | solution.py:31
  22.6 12.9 %collective-permute-start.7 = (bf16[16,112,128]{2,1,0:T(8,128)(2,1)S(1)}, bf16[16,112,128]{2,1,0:T(8,128)(2,1)S(1)}, u32[]{:S(2)}, u32[]{:S(2)}) collective-permute-start(bf16[16,112,128]{2,1,0:T(8,128)(2,1)S(1)} %get-tuple-element.34.refs_1_), channel_id=1, source_target_pairs={{0,24},{8,0},{16,8},{24,16},{32,56},{40,32},{48,40},{56,48},{64,88... | collective-permute-start | bytes 1376264 | tf_op jit(solution)/shard_map/ppermute | solution.py:32
  24.8 24.3 %collective-permute-start.11 = (bf16[16,112,128]{2,1,0:T(8,128)(2,1)S(1)}, bf16[16,112,128]{2,1,0:T(8,128)(2,1)S(1)}, u32[]{:S(2)}, u32[]{:S(2)}) collective-permute-start(bf16[16,112,128]{2,1,0:T(8,128)(2,1)S(1)} %get-tuple-element.33.refs_0_), channel_id=1, source_target_pairs={{0,24},{8,0},{16,8},{24,16},{32,56},{40,32},{48,40},{56,48},{64,88... | collective-permute-start | bytes 1376264 | tf_op jit(solution)/shard_map/ppermute | solution.py:34
  26.2 23.0 %collective-permute-start.10 = (bf16[16,112,128]{2,1,0:T(8,128)(2,1)S(1)}, bf16[16,112,128]{2,1,0:T(8,128)(2,1)S(1)}, u32[]{:S(2)}, u32[]{:S(2)}) collective-permute-start(bf16[16,112,128]{2,1,0:T(8,128)(2,1)S(1)} %get-tuple-element.34.refs_1_), channel_id=1, source_target_pairs={{0,8},{8,16},{16,24},{24,0},{32,40},{40,48},{48,56},{56,32},{64,72... | collective-permute-start | bytes 1376264 | tf_op jit(solution)/shard_map/ppermute | solution.py:33
  35.6 23.3 %collective-permute-start.8 = (bf16[16,112,128]{2,1,0:T(8,128)(2,1)S(1)}, bf16[16,112,128]{2,1,0:T(8,128)(2,1)S(1)}, u32[]{:S(2)}, u32[]{:S(2)}) collective-permute-start(bf16[16,112,128]{2,1,0:T(8,128)(2,1)S(1)} %get-tuple-element.36.refs_0_), channel_id=1, source_target_pairs={{0,8},{8,16},{16,24},{24,0},{32,40},{40,48},{48,56},{56,32},{64,72... | collective-permute-start | bytes 1376264 | tf_op jit(solution)/shard_map/ppermute | solution.py:37
  36.7 22.2 %collective-permute-start.9 = (bf16[16,112,128]{2,1,0:T(8,128)(2,1)S(1)}, bf16[16,112,128]{2,1,0:T(8,128)(2,1)S(1)}, u32[]{:S(2)}, u32[]{:S(2)}) collective-permute-start(bf16[16,112,128]{2,1,0:T(8,128)(2,1)S(1)} %get-tuple-element.37.refs_1_), channel_id=1, source_target_pairs={{0,24},{8,0},{16,8},{24,16},{32,56},{40,32},{48,40},{56,48},{64,88... | collective-permute-start | bytes 1376264 | tf_op jit(solution)/shard_map/ppermute | solution.py:38
  58.8 0.8 copy-start
  58.9 0.9 copy-start.1
  68.4 12.7 %collective-permute-start.12 = (bf16[24,32,128]{2,1,0:T(8,128)(2,1)S(1)}, bf16[24,32,128]{2,1,0:T(8,128)(2,1)S(1)}, u32[]{:S(2)}, u32[]{:S(2)}) collective-permute-start(bf16[24,32,128]{2,1,0:T(8,128)(2,1)S(1)} %get-tuple-element.42), channel_id=1, source_target_pairs={{0,1},{1,2},{2,3},{3,4},{4,5},{5,6},{6,7},{7,0},{8,9},{9,10},{10,1... | collective-permute-start | bytes 589832 | tf_op jit(solution)/shard_map/ppermute | solution.py:368
  72.0 12.0 %collective-permute-start.13 = (bf16[24,32,128]{2,1,0:T(8,128)(2,1)S(1)}, bf16[24,32,128]{2,1,0:T(8,128)(2,1)S(1)}, u32[]{:S(2)}, u32[]{:S(2)}) collective-permute-start(bf16[24,32,128]{2,1,0:T(8,128)(2,1)S(1)} %get-tuple-element.43), channel_id=1, source_target_pairs={{0,2},{1,3},{2,4},{3,5},{4,6},{5,7},{6,0},{7,1},{8,10},{9,11},{10,... | collective-permute-start | bytes 589832 | tf_op jit(solution)/shard_map/ppermute | solution.py:368
  73.3 12.2 %collective-permute-start.14 = (bf16[24,32,128]{2,1,0:T(8,128)(2,1)S(1)}, bf16[24,32,128]{2,1,0:T(8,128)(2,1)S(1)}, u32[]{:S(2)}, u32[]{:S(2)}) collective-permute-start(bf16[24,32,128]{2,1,0:T(8,128)(2,1)S(1)} %get-tuple-element.44), channel_id=1, source_target_pairs={{0,3},{1,4},{2,5},{3,6},{4,7},{5,0},{6,1},{7,2},{8,11},{9,12},{10,... | collective-permute-start | bytes 589832 | tf_op jit(solution)/shard_map/ppermute | solution.py:368
  78.8 16.8 %collective-permute-start.15 = (bf16[24,32,128]{2,1,0:T(8,128)(2,1)S(1)}, bf16[24,32,128]{2,1,0:T(8,128)(2,1)S(1)}, u32[]{:S(2)}, u32[]{:S(2)}) collective-permute-start(bf16[24,32,128]{2,1,0:T(8,128)(2,1)S(1)} %get-tuple-element.45), channel_id=1, source_target_pairs={{0,4},{1,5},{2,6},{3,7},{4,0},{5,1},{6,2},{7,3},{8,12},{9,13},{10,... | collective-permute-start | bytes 589832 | tf_op jit(solution)/shard_map/ppermute | solution.py:368
  78.8 17.4 %collective-permute-start.16 = (bf16[24,32,128]{2,1,0:T(8,128)(2,1)S(1)}, bf16[24,32,128]{2,1,0:T(8,128)(2,1)S(1)}, u32[]{:S(2)}, u32[]{:S(2)}) collective-permute-start(bf16[24,32,128]{2,1,0:T(8,128)(2,1)S(1)} %get-tuple-element.46), channel_id=1, source_target_pairs={{0,5},{1,6},{2,7},{3,0},{4,1},{5,2},{6,3},{7,4},{8,13},{9,14},{10,... | collective-permute-start | bytes 589832 | tf_op jit(solution)/shard_map/ppermute | solution.py:368
  81.1 15.1 %collective-permute-start.17 = (bf16[24,32,128]{2,1,0:T(8,128)(2,1)S(1)}, bf16[24,32,128]{2,1,0:T(8,128)(2,1)S(1)}, u32[]{:S(2)}, u32[]{:S(2)}) collective-permute-start(bf16[24,32,128]{2,1,0:T(8,128)(2,1)S(1)} %get-tuple-element.47), channel_id=1, source_target_pairs={{0,6},{1,7},{2,0},{3,1},{4,2},{5,3},{6,4},{7,5},{8,14},{9,15},{10,... | collective-permute-start | bytes 589832 | tf_op jit(solution)/shard_map/ppermute | solution.py:368
  84.0 12.2 %collective-permute-start.18 = (bf16[24,32,128]{2,1,0:T(8,128)(2,1)}, bf16[24,32,128]{2,1,0:T(8,128)(2,1)S(1)}, u32[]{:S(2)}, u32[]{:S(2)}) collective-permute-start(bf16[24,32,128]{2,1,0:T(8,128)(2,1)} %get-tuple-element.48), channel_id=1, source_target_pairs={{0,7},{1,0},{2,1},{3,2},{4,3},{5,4},{6,5},{7,6},{8,15},{9,8},{10,9... | collective-permute-start | bytes 589832 | tf_op jit(solution)/shard_map/ppermute | solution.py:368
